TPU v7x, 256 devices: a whole 4x4x8 slice. The times are simulated.
256 devices in a mesh: dp: 64 (over z, x, core), branch: 4 (over y).
Axes of the slice: x: 4, y: 4, z: 8, core: 2. Of those that a mesh axis runs over, the one named last changes fastest.
Arguments:
- prefix_keys: bfloat16 [64, 4, 512, 512], P('dp', 'branch'), may hold values from -6 to 6
- prefix_values: bfloat16 [64, 4, 512, 512], P('dp', 'branch'), may hold values from -6 to 6
- resp_query: bfloat16 [64, 4, 8, 32, 4096], P('dp', 'branch'), may hold values from -6 to 6
- resp_keys: bfloat16 [64, 4, 8, 32, 512], P('dp', 'branch'), may hold values from -6 to 6
- resp_values: bfloat16 [64, 4, 8, 32, 512], P('dp', 'branch'), may hold values from -6 to 6
- out_grad: bfloat16 [64, 4, 8, 32, 4096], P('dp', 'branch'), may hold values from -6 to 6
- q_gain: float32 [128], replicated, may hold values from 0.1 to 1.9
- k_gain: float32 [128], replicated, may hold values from 0.1 to 1.9
- lengths: int32 [64, 4, 8], P('dp', 'branch'), may hold values from 1 to 32, as said below
- slot_prompt: int32 [64, 4, 8], P('dp', 'branch'), may hold values from 0 to 3, as said below
- prefix_owner: int32 [64, 4], P('dp'), may hold values from 0 to 3, as said below
Outputs:
- attended: bfloat16 [64, 4, 8, 32, 4096], P('dp', 'branch')
- d_query: bfloat16 [64, 4, 8, 32, 4096], P('dp', 'branch')
- d_resp_keys: bfloat16 [64, 4, 8, 32, 512], P('dp', 'branch')
- d_resp_values: bfloat16 [64, 4, 8, 32, 512], P('dp', 'branch')
- d_prefix_keys: bfloat16 [64, 4, 512, 512], P('dp', 'branch')
- d_prefix_values: bfloat16 [64, 4, 512, 512], P('dp', 'branch')
- q_gain_grad: float32 [128], replicated
- k_gain_grad: float32 [128], replicated
Inputs may be any that keep to these rules, and one draw needn't show every extreme that they name: `lengths`: every device has a slot whose length is exactly 32. `slot_prompt`: each prompt of a group is answered by exactly 8 slots of the group, none on the device that holds its prefix. `prefix_owner`: each row is a permutation of the group's devices.
All inputs are finite; a program needn't handle non-finite values.
Results may differ from a plain program's by a relative error of at most 0.014.
Values may be sent and summed in bfloat16 or wider, within the bound.
A program may use at most 128 MiB of HBM per device.

v0:
```python
import math

import jax
import jax.numpy as jnp
from jax import lax
from jax.sharding import PartitionSpec as P

EPSILON = 1e-06


def product(pattern, first_op, second_op):
    return jnp.einsum(pattern, first_op, second_op, preferred_element_type=jnp.float32)


def norm_forward(raw_vals, gain_vec):
    inv_rms = lax.rsqrt(jnp.mean(raw_vals * raw_vals, axis=-1, keepdims=True) + EPSILON)
    normed = raw_vals * inv_rms
    return ((normed * gain_vec).astype(jnp.bfloat16), normed, inv_rms)


def norm_backward(grad_hat, normed, inv_rms, gain_vec):
    scaled_grad = grad_hat * gain_vec
    grad_raw = inv_rms * (
        scaled_grad - normed * jnp.mean(scaled_grad * normed, axis=-1, keepdims=True)
    )
    gain_grad = jnp.sum(grad_hat * normed, axis=tuple(range(grad_hat.ndim - 1)))
    return (grad_raw, gain_grad)


def slot_pass(queries, resp_k, resp_v, grad_in, length, pre_k, pre_v, q_gain, k_gain):
    head_size = q_gain.shape[0]
    resp_len = queries.shape[0]
    q_heads = queries.shape[1] // head_size
    kv_heads = resp_k.shape[1] // head_size
    group_size = q_heads // kv_heads
    pre_len = pre_k.shape[0]
    q_hat, q_normed, q_inv = norm_forward(
        queries.astype(jnp.float32).reshape(resp_len, q_heads, head_size), q_gain
    )
    k_hat, k_normed, k_inv = norm_forward(
        resp_k.astype(jnp.float32).reshape(resp_len, kv_heads, head_size), k_gain
    )
    all_keys = jnp.concatenate([pre_k.reshape(pre_len, kv_heads, head_size), k_hat], axis=0)
    all_vals = jnp.concatenate(
        [
            pre_v.reshape(pre_len, kv_heads, head_size),
            resp_v.reshape(resp_len, kv_heads, head_size),
        ],
        axis=0,
    )
    grouped_q = q_hat.reshape(resp_len, kv_heads, group_size, head_size)
    score_scale = 1.0 / math.sqrt(head_size)
    row_pos = jnp.arange(resp_len, dtype=jnp.int32)
    key_pos = jnp.arange(pre_len + resp_len, dtype=jnp.int32)
    allowed = (key_pos[None, :] < pre_len) | (key_pos[None, :] - pre_len <= row_pos[:, None])
    raw_scores = product("rhgd,jhd->hrgj", grouped_q, all_keys) * score_scale
    raw_scores = jnp.where(allowed[None, :, None, :], raw_scores, -1e30)
    row_peak = jnp.max(raw_scores, axis=-1, keepdims=True)
    shifted = jnp.exp(raw_scores - row_peak)
    attn_probs = shifted / jnp.sum(shifted, axis=-1, keepdims=True)
    probs_low = attn_probs.astype(jnp.bfloat16)
    live_rows = row_pos < length
    mixed = product("hrgj,jhd->rhgd", probs_low, all_vals).reshape(resp_len, q_heads * head_size)
    attended = jnp.where(live_rows[:, None], mixed, 0.0).astype(jnp.bfloat16)
    grad_out = jnp.where(live_rows[:, None], grad_in, jnp.zeros_like(grad_in)).reshape(
        resp_len, kv_heads, group_size, head_size
    )
    grad_prob = product("rhgd,jhd->hrgj", grad_out, all_vals)
    row_total = jnp.sum(attn_probs * grad_prob, axis=-1, keepdims=True)
    grad_score = (attn_probs * (grad_prob - row_total) * score_scale).astype(jnp.bfloat16)
    grad_q_hat = product("hrgj,jhd->rhgd", grad_score, all_keys).reshape(
        resp_len, q_heads, head_size
    )
    grad_keys = product("hrgj,rhgd->jhd", grad_score, grouped_q)
    grad_vals = product("hrgj,rhgd->jhd", probs_low, grad_out)
    grad_q, q_gain_part = norm_backward(grad_q_hat, q_normed, q_inv, q_gain)
    grad_k, k_gain_part = norm_backward(grad_keys[pre_len:], k_normed, k_inv, k_gain)
    return (
        attended,
        grad_q.reshape(resp_len, -1).astype(jnp.bfloat16),
        grad_k.reshape(resp_len, -1).astype(jnp.bfloat16),
        grad_vals[pre_len:].reshape(resp_len, -1).astype(jnp.bfloat16),
        grad_keys[:pre_len].reshape(pre_len, -1),
        grad_vals[:pre_len].reshape(pre_len, -1),
        q_gain_part,
        k_gain_part,
    )


def device_pass(
    queries, resp_k, resp_v, grad_in, slot_lengths, owners, all_pre_k, all_pre_v, q_gain, k_gain
):
    owner_count, pre_len, kv_width = all_pre_k.shape
    head_size = q_gain.shape[0]
    start = (
        jnp.zeros((owner_count, pre_len, kv_width), jnp.float32),
        jnp.zeros((owner_count, pre_len, kv_width), jnp.float32),
        jnp.zeros((head_size,), jnp.float32),
        jnp.zeros((head_size,), jnp.float32),
    )

    def step(carry, inputs):
        slot_q, slot_k, slot_v, slot_g, length, owner = inputs
        pre_k = lax.dynamic_index_in_dim(all_pre_k, owner, 0, keepdims=False)
        pre_v = lax.dynamic_index_in_dim(all_pre_v, owner, 0, keepdims=False)
        results = slot_pass(slot_q, slot_k, slot_v, slot_g, length, pre_k, pre_v, q_gain, k_gain)
        acc_k, acc_v, q_acc, k_acc = carry
        acc_k = lax.dynamic_update_index_in_dim(
            acc_k, lax.dynamic_index_in_dim(acc_k, owner, 0, keepdims=False) + results[4], owner, 0
        )
        acc_v = lax.dynamic_update_index_in_dim(
            acc_v, lax.dynamic_index_in_dim(acc_v, owner, 0, keepdims=False) + results[5], owner, 0
        )
        return ((acc_k, acc_v, q_acc + results[6], k_acc + results[7]), results[:4])

    carry, stacked = lax.scan(step, start, (queries, resp_k, resp_v, grad_in, slot_lengths, owners))
    return (stacked, carry)


def body(
    prefix_keys,
    prefix_values,
    resp_query,
    resp_keys,
    resp_values,
    out_grad,
    q_gain,
    k_gain,
    lengths,
    slot_prompt,
    prefix_owner,
):
    head_size = q_gain.shape[0]
    pre_len = prefix_keys.shape[2]
    kv_width = prefix_keys.shape[3]
    kv_heads = kv_width // head_size
    own_keys = prefix_keys[0, 0].astype(jnp.float32).reshape(pre_len, kv_heads, head_size)
    own_hat, own_normed, own_inv = norm_forward(own_keys, k_gain)
    sent_keys = own_hat.reshape(1, 1, pre_len, kv_width)
    all_pre_k, all_pre_v = (
        lax.all_gather(sent_keys, "branch", axis=1, tiled=True),
        lax.all_gather(prefix_values, "branch", axis=1, tiled=True),
    )
    prompt_ids = slot_prompt[0, 0]
    owner_table = prefix_owner[0]
    member_ids = jnp.arange(owner_table.shape[0], dtype=jnp.int32)
    owners = jnp.sum(
        jnp.where(prompt_ids[:, None] == member_ids[None, :], owner_table[None, :], 0), axis=1
    )
    stacked, carry = device_pass(
        resp_query[0, 0],
        resp_keys[0, 0],
        resp_values[0, 0],
        out_grad[0, 0],
        lengths[0, 0],
        owners,
        all_pre_k[0],
        all_pre_v[0],
        q_gain,
        k_gain,
    )
    part_k, part_v, q_gain_part, k_gain_part = carry
    summed_k, summed_v = (
        lax.psum_scatter(
            part_k.astype(jnp.bfloat16), "branch", scatter_dimension=0, tiled=True
        ).astype(jnp.float32),
        lax.psum_scatter(
            part_v.astype(jnp.bfloat16), "branch", scatter_dimension=0, tiled=True
        ).astype(jnp.float32),
    )
    summed_k = summed_k[0]
    summed_v = summed_v[0]
    grad_own, own_gain_part = norm_backward(
        summed_k.reshape(pre_len, kv_heads, head_size), own_normed, own_inv, k_gain
    )
    k_local = k_gain_part + own_gain_part
    q_grad_all, k_grad_all = lax.psum((q_gain_part, k_local), ("dp", "branch"))
    return (
        stacked[0][None, None],
        stacked[1][None, None],
        stacked[2][None, None],
        stacked[3][None, None],
        grad_own.reshape(1, 1, pre_len, kv_width).astype(jnp.bfloat16),
        summed_v.reshape(1, 1, pre_len, kv_width).astype(jnp.bfloat16),
        q_grad_all,
        k_grad_all,
    )


def solution(mesh):
    return jax.shard_map(
        body,
        mesh=mesh,
        in_specs=(
            P("dp", "branch", None, None),
            P("dp", "branch", None, None),
            P("dp", "branch", None, None, None),
            P("dp", "branch", None, None, None),
            P("dp", "branch", None, None, None),
            P("dp", "branch", None, None, None),
            P(),
            P(),
            P("dp", "branch", None),
            P("dp", "branch", None),
            P("dp", None),
        ),
        out_specs=(
            P("dp", "branch", None, None, None),
            P("dp", "branch", None, None, None),
            P("dp", "branch", None, None, None),
            P("dp", "branch", None, None, None),
            P("dp", "branch", None, None),
            P("dp", "branch", None, None),
            P(),
            P(),
        ),
        check_vma=False,
    )
```

profile of v0, /device:TPU:8, one launch (start us, length us, event | category | flops | bytes accessed | tf_op | source)
XLA Modules:
  0.0 711.6 jit_solution(14460288217346883863)
XLA Ops:
  13.6 31.5 %all-gather.5.cloned.1.call-done = bf16[1,4,512,512]{3,2,0,1:T(8,128)(2,1)} async-done(((bf16[1,1,512,512]{3,2,0,1:T(8,128)(2,1)}), bf16[1,4,512,512]{3,2,0,1:T(8,128)(2,1)}) %all-gather.5.cloned.1.call-update) | async-done | bytes 2097168 | tf_op jit(solution)/shard_map/all_gather | solution.py:142
  45.2 35.9 %all-gather.3.cloned.1.call-done = bf16[1,4,512,512]{3,2,0,1:T(8,128)(2,1)} async-done(((bf16[1,1,512,512]{3,2,0,1:T(8,128)(2,1)}), bf16[1,4,512,512]{3,2,0,1:T(8,128)(2,1)}) %all-gather.3.cloned.1.call-update) | async-done | bytes 2097168 | tf_op jit(solution)/shard_map/all_gather | solution.py:141
  81.0 2.5 broadcast.322.clone2
  83.6 2.5 broadcast.322.clone
  86.0 495.9 %while.27 = (s32[]{:T(128)}, f32[4,512,512]{2,1,0:T(8,128)}, f32[4,512,512]{2,1,0:T(8,128)}, f32[128]{0:T(128)}, f32[128]{0:T(128)}, /*index=5*/bf16[8,32,4096]{...) while((s32[]{:T(128)}, f32[4,512,512]{2,1,0:T(8,128)}, ...), condition=%wide.region_12.13_spmd.clone, body=%wide.region_2.12_spmd.clone.sunk | while | flops 871209472 | bytes 106266848 | solution.py:116
  105.5 2.7 fusion.85
  108.2 10.0 %multiply_convert_fusion.11 = bf16[4,32,8,544]{3,2,1,0:T(8,128)(2,1)S(1)} fusion(f32[4,32,8,544]{3,2,1,0:T(8,128)} %fusion.83, f32[4,32,8,544]{3,2,1,0:T(8,128)} %get-tuple-element.662, f32[4,32,8]{2,1,0:T(8,128)S(1)} %get-tuple-element.663), kind=kOutput, calls=%fused_computation.2.clone.1 | output fusion | flops 3900959 | bytes 5574656 | tf_op jit(solution)/shard_map/while/body/eval_jaxpr/sub | solution.py:70
  130.0 2.7 copy.307
  132.7 2.4 bitcast_add_fusion.4
  135.1 2.6 copy.308
  166.9 2.7 fusion.85
  169.6 10.0 %multiply_convert_fusion.11 = bf16[4,32,8,544]{3,2,1,0:T(8,128)(2,1)S(1)} fusion(f32[4,32,8,544]{3,2,1,0:T(8,128)} %fusion.83, f32[4,32,8,544]{3,2,1,0:T(8,128)} %get-tuple-element.662, f32[4,32,8]{2,1,0:T(8,128)S(1)} %get-tuple-element.663), kind=kOutput, calls=%fused_computation.2.clone.1 | output fusion | flops 3900959 | bytes 5574656 | tf_op jit(solution)/shard_map/while/body/eval_jaxpr/sub | solution.py:70
  192.0 2.7 copy.307
  194.7 2.4 bitcast_add_fusion.4
  197.1 2.6 copy.308
  228.9 2.7 fusion.85
  231.6 10.0 %multiply_convert_fusion.11 = bf16[4,32,8,544]{3,2,1,0:T(8,128)(2,1)S(1)} fusion(f32[4,32,8,544]{3,2,1,0:T(8,128)} %fusion.83, f32[4,32,8,544]{3,2,1,0:T(8,128)} %get-tuple-element.662, f32[4,32,8]{2,1,0:T(8,128)S(1)} %get-tuple-element.663), kind=kOutput, calls=%fused_computation.2.clone.1 | output fusion | flops 3900959 | bytes 5574656 | tf_op jit(solution)/shard_map/while/body/eval_jaxpr/sub | solution.py:70
  254.1 2.7 copy.307
  256.8 2.4 bitcast_add_fusion.4
  259.2 2.6 copy.308
  290.9 2.7 fusion.85
  293.7 10.0 %multiply_convert_fusion.11 = bf16[4,32,8,544]{3,2,1,0:T(8,128)(2,1)S(1)} fusion(f32[4,32,8,544]{3,2,1,0:T(8,128)} %fusion.83, f32[4,32,8,544]{3,2,1,0:T(8,128)} %get-tuple-element.662, f32[4,32,8]{2,1,0:T(8,128)S(1)} %get-tuple-element.663), kind=kOutput, calls=%fused_computation.2.clone.1 | output fusion | flops 3900959 | bytes 5574656 | tf_op jit(solution)/shard_map/while/body/eval_jaxpr/sub | solution.py:70
  316.1 2.7 copy.307
  318.8 2.4 bitcast_add_fusion.4
  321.2 2.6 copy.308
  353.0 2.7 fusion.85
  355.8 10.0 %multiply_convert_fusion.11 = bf16[4,32,8,544]{3,2,1,0:T(8,128)(2,1)S(1)} fusion(f32[4,32,8,544]{3,2,1,0:T(8,128)} %fusion.83, f32[4,32,8,544]{3,2,1,0:T(8,128)} %get-tuple-element.662, f32[4,32,8]{2,1,0:T(8,128)S(1)} %get-tuple-element.663), kind=kOutput, calls=%fused_computation.2.clone.1 | output fusion | flops 3900959 | bytes 5574656 | tf_op jit(solution)/shard_map/while/body/eval_jaxpr/sub | solution.py:70
  378.2 2.7 copy.307
  380.9 2.4 bitcast_add_fusion.4
  383.3 2.6 copy.308
  415.0 2.7 fusion.85
  417.8 10.0 %multiply_convert_fusion.11 = bf16[4,32,8,544]{3,2,1,0:T(8,128)(2,1)S(1)} fusion(f32[4,32,8,544]{3,2,1,0:T(8,128)} %fusion.83, f32[4,32,8,544]{3,2,1,0:T(8,128)} %get-tuple-element.662, f32[4,32,8]{2,1,0:T(8,128)S(1)} %get-tuple-element.663), kind=kOutput, calls=%fused_computation.2.clone.1 | output fusion | flops 3900959 | bytes 5574656 | tf_op jit(solution)/shard_map/while/body/eval_jaxpr/sub | solution.py:70
  440.2 2.7 copy.307
  442.9 2.4 bitcast_add_fusion.4
  445.3 2.6 copy.308
  477.1 2.7 fusion.85
  479.9 10.0 %multiply_convert_fusion.11 = bf16[4,32,8,544]{3,2,1,0:T(8,128)(2,1)S(1)} fusion(f32[4,32,8,544]{3,2,1,0:T(8,128)} %fusion.83, f32[4,32,8,544]{3,2,1,0:T(8,128)} %get-tuple-element.662, f32[4,32,8]{2,1,0:T(8,128)S(1)} %get-tuple-element.663), kind=kOutput, calls=%fused_computation.2.clone.1 | output fusion | flops 3900959 | bytes 5574656 | tf_op jit(solution)/shard_map/while/body/eval_jaxpr/sub | solution.py:70
  502.3 2.7 copy.307
  505.0 2.4 bitcast_add_fusion.4
  507.4 2.6 copy.308
  539.1 2.7 fusion.85
  541.9 10.0 %multiply_convert_fusion.11 = bf16[4,32,8,544]{3,2,1,0:T(8,128)(2,1)S(1)} fusion(f32[4,32,8,544]{3,2,1,0:T(8,128)} %fusion.83, f32[4,32,8,544]{3,2,1,0:T(8,128)} %get-tuple-element.662, f32[4,32,8]{2,1,0:T(8,128)S(1)} %get-tuple-element.663), kind=kOutput, calls=%fused_computation.2.clone.1 | output fusion | flops 3900959 | bytes 5574656 | tf_op jit(solution)/shard_map/while/body/eval_jaxpr/sub | solution.py:70
  564.3 2.7 copy.307
  569.4 2.6 copy.308
  582.0 3.8 convert_element_type.186
  585.9 3.8 convert_element_type.189
  592.3 25.8 %reduce-scatter.3.cloned.1.call-done = bf16[1,512,512]{2,1,0:T(8,128)(2,1)} async-done(((bf16[4,512,512]{2,1,0:T(8,128)(2,1)}), bf16[1,512,512]{2,1,0:T(8,128)(2,1)}) %reduce-scatter.3.cloned.1.call-update) | async-done | bytes 524304 | tf_op jit(solution)/shard_map/reduce_scatter | solution.py:164
  625.9 78.0 %all-reduce = (f32[128]{0:T(128)}, f32[128]{0:T(128)}) all-reduce(f32[128]{0:T(128)S(1)} %copy-done.36, f32[128]{0:T(128)S(1)} %add.105), channel_id=1, replica_groups=mesh['dp'=64,'branch'=4] {'dp','branch'}, use_global_device_ids=true, to_apply=%region_16.17 | all-reduce | flops 256 | bytes 2048 | tf_op jit(solution)/shard_map/psum | solution.py:177
  (995 shorter events, 332.4 us)
Async XLA Ops:
  7.2 38.0 %all-gather.5.cloned.1.call-start = ((), (), s32[]{:S(2)}) async-start(), calls=%async_computation.3 | async-start | bytes 2621440 | tf_op jit(solution)/shard_map/all_gather | solution.py:142
  7.9 73.1 %all-gather.3.cloned.1.call-start = ((), (), s32[]{:S(2)}) async-start(), calls=%async_computation.2 | async-start | bytes 2621440 | tf_op jit(solution)/shard_map/all_gather | solution.py:141
  12.2 71.3 %copy-start.9 = (f32[1,1,512,512]{3,2,0,1:T(8,128)}, f32[1,1,512,512]{3,2,0,1:T(8,128)S(1)}, u32[]{:S(2)}) copy-start(f32[1,1,512,512]{3,2,0,1:T(8,128)S(1)} %mul.336) | copy-start | bytes 3145732
  12.3 71.3 %copy-start.33 = (f32[512]{0:T(512)}, f32[512]{0:T(512)S(1)}, u32[]{:S(2)}) copy-start(f32[512]{0:T(512)S(1)} %broadcast_bitcast_fusion.1) | copy-start | bytes 6148
  13.4 604.6 %reduce-scatter.3.cloned.1.call-start = ((), (), s32[]{:S(2)}) async-start(), calls=%async_computation.4 | async-start | bytes 2621440 | tf_op jit(solution)/shard_map/reduce_scatter | solution.py:164
  86.0 6.9 copy-start.41
  89.8 13.5 %copy-start.28 = (pred[32]{0:T(512)(128)(4,1)}, pred[32]{0:T(512)(128)(4,1)S(1)}, u32[]{:S(2)}) copy-start(pred[32]{0:T(512)(128)(4,1)S(1)} %iota_compare_fusion.6) | copy-start | bytes 100 | tf_op jit(solution)/shard_map/while
  90.7 12.6 %copy-start.18 = (bf16[32,4,128]{2,0,1:T(8,128)(2,1)}, bf16[32,4,128]{2,0,1:T(8,128)(2,1)S(1)}, u32[]{:S(2)}) copy-start(bf16[32,4,128]{2,0,1:T(8,128)(2,1)S(1)} %copy.300) | copy-start | bytes 98308 | tf_op jit(solution)/shard_map/while
  108.2 10.0 %copy-start.2 = (f32[4,32,8,544]{3,2,1,0:T(8,128)S(1)}, f32[4,32,8,544]{3,2,1,0:T(8,128)}, u32[]{:S(2)}) copy-start(f32[4,32,8,544]{3,2,1,0:T(8,128)} %get-tuple-element.662) | copy-start | bytes 6684676 | tf_op jit(solution)/shard_map/while
  132.7 5.0 copy-start.20
  147.4 6.9 copy-start.41
  151.2 13.5 %copy-start.28 = (pred[32]{0:T(512)(128)(4,1)}, pred[32]{0:T(512)(128)(4,1)S(1)}, u32[]{:S(2)}) copy-start(pred[32]{0:T(512)(128)(4,1)S(1)} %iota_compare_fusion.6) | copy-start | bytes 100 | tf_op jit(solution)/shard_map/while
  152.1 12.6 %copy-start.18 = (bf16[32,4,128]{2,0,1:T(8,128)(2,1)}, bf16[32,4,128]{2,0,1:T(8,128)(2,1)S(1)}, u32[]{:S(2)}) copy-start(bf16[32,4,128]{2,0,1:T(8,128)(2,1)S(1)} %copy.300) | copy-start | bytes 98308 | tf_op jit(solution)/shard_map/while
  169.6 10.0 %copy-start.2 = (f32[4,32,8,544]{3,2,1,0:T(8,128)S(1)}, f32[4,32,8,544]{3,2,1,0:T(8,128)}, u32[]{:S(2)}) copy-start(f32[4,32,8,544]{3,2,1,0:T(8,128)} %get-tuple-element.662) | copy-start | bytes 6684676 | tf_op jit(solution)/shard_map/while
  194.7 5.0 copy-start.20
  209.5 6.9 copy-start.41
  213.3 13.5 %copy-start.28 = (pred[32]{0:T(512)(128)(4,1)}, pred[32]{0:T(512)(128)(4,1)S(1)}, u32[]{:S(2)}) copy-start(pred[32]{0:T(512)(128)(4,1)S(1)} %iota_compare_fusion.6) | copy-start | bytes 100 | tf_op jit(solution)/shard_map/while
  214.1 12.6 %copy-start.18 = (bf16[32,4,128]{2,0,1:T(8,128)(2,1)}, bf16[32,4,128]{2,0,1:T(8,128)(2,1)S(1)}, u32[]{:S(2)}) copy-start(bf16[32,4,128]{2,0,1:T(8,128)(2,1)S(1)} %copy.300) | copy-start | bytes 98308 | tf_op jit(solution)/shard_map/while
  231.6 10.0 %copy-start.2 = (f32[4,32,8,544]{3,2,1,0:T(8,128)S(1)}, f32[4,32,8,544]{3,2,1,0:T(8,128)}, u32[]{:S(2)}) copy-start(f32[4,32,8,544]{3,2,1,0:T(8,128)} %get-tuple-element.662) | copy-start | bytes 6684676 | tf_op jit(solution)/shard_map/while
  271.5 6.9 copy-start.41
  275.3 13.5 %copy-start.28 = (pred[32]{0:T(512)(128)(4,1)}, pred[32]{0:T(512)(128)(4,1)S(1)}, u32[]{:S(2)}) copy-start(pred[32]{0:T(512)(128)(4,1)S(1)} %iota_compare_fusion.6) | copy-start | bytes 100 | tf_op jit(solution)/shard_map/while
  276.2 12.6 %copy-start.18 = (bf16[32,4,128]{2,0,1:T(8,128)(2,1)}, bf16[32,4,128]{2,0,1:T(8,128)(2,1)S(1)}, u32[]{:S(2)}) copy-start(bf16[32,4,128]{2,0,1:T(8,128)(2,1)S(1)} %copy.300) | copy-start | bytes 98308 | tf_op jit(solution)/shard_map/while
  293.7 10.0 %copy-start.2 = (f32[4,32,8,544]{3,2,1,0:T(8,128)S(1)}, f32[4,32,8,544]{3,2,1,0:T(8,128)}, u32[]{:S(2)}) copy-start(f32[4,32,8,544]{3,2,1,0:T(8,128)} %get-tuple-element.662) | copy-start | bytes 6684676 | tf_op jit(solution)/shard_map/while
  318.8 5.0 copy-start.20
  333.6 6.9 copy-start.41
  337.4 13.5 %copy-start.28 = (pred[32]{0:T(512)(128)(4,1)}, pred[32]{0:T(512)(128)(4,1)S(1)}, u32[]{:S(2)}) copy-start(pred[32]{0:T(512)(128)(4,1)S(1)} %iota_compare_fusion.6) | copy-start | bytes 100 | tf_op jit(solution)/shard_map/while
  338.3 12.6 %copy-start.18 = (bf16[32,4,128]{2,0,1:T(8,128)(2,1)}, bf16[32,4,128]{2,0,1:T(8,128)(2,1)S(1)}, u32[]{:S(2)}) copy-start(bf16[32,4,128]{2,0,1:T(8,128)(2,1)S(1)} %copy.300) | copy-start | bytes 98308 | tf_op jit(solution)/shard_map/while
  355.8 10.0 %copy-start.2 = (f32[4,32,8,544]{3,2,1,0:T(8,128)S(1)}, f32[4,32,8,544]{3,2,1,0:T(8,128)}, u32[]{:S(2)}) copy-start(f32[4,32,8,544]{3,2,1,0:T(8,128)} %get-tuple-element.662) | copy-start | bytes 6684676 | tf_op jit(solution)/shard_map/while
  395.6 6.9 copy-start.41
  399.4 13.5 %copy-start.28 = (pred[32]{0:T(512)(128)(4,1)}, pred[32]{0:T(512)(128)(4,1)S(1)}, u32[]{:S(2)}) copy-start(pred[32]{0:T(512)(128)(4,1)S(1)} %iota_compare_fusion.6) | copy-start | bytes 100 | tf_op jit(solution)/shard_map/while
  400.3 12.6 %copy-start.18 = (bf16[32,4,128]{2,0,1:T(8,128)(2,1)}, bf16[32,4,128]{2,0,1:T(8,128)(2,1)S(1)}, u32[]{:S(2)}) copy-start(bf16[32,4,128]{2,0,1:T(8,128)(2,1)S(1)} %copy.300) | copy-start | bytes 98308 | tf_op jit(solution)/shard_map/while
  417.8 10.0 %copy-start.2 = (f32[4,32,8,544]{3,2,1,0:T(8,128)S(1)}, f32[4,32,8,544]{3,2,1,0:T(8,128)}, u32[]{:S(2)}) copy-start(f32[4,32,8,544]{3,2,1,0:T(8,128)} %get-tuple-element.662) | copy-start | bytes 6684676 | tf_op jit(solution)/shard_map/while
  442.9 5.0 copy-start.20
  457.7 6.9 copy-start.41
  461.5 13.5 %copy-start.28 = (pred[32]{0:T(512)(128)(4,1)}, pred[32]{0:T(512)(128)(4,1)S(1)}, u32[]{:S(2)}) copy-start(pred[32]{0:T(512)(128)(4,1)S(1)} %iota_compare_fusion.6) | copy-start | bytes 100 | tf_op jit(solution)/shard_map/while
  462.4 12.6 %copy-start.18 = (bf16[32,4,128]{2,0,1:T(8,128)(2,1)}, bf16[32,4,128]{2,0,1:T(8,128)(2,1)S(1)}, u32[]{:S(2)}) copy-start(bf16[32,4,128]{2,0,1:T(8,128)(2,1)S(1)} %copy.300) | copy-start | bytes 98308 | tf_op jit(solution)/shard_map/while
  479.9 10.0 %copy-start.2 = (f32[4,32,8,544]{3,2,1,0:T(8,128)S(1)}, f32[4,32,8,544]{3,2,1,0:T(8,128)}, u32[]{:S(2)}) copy-start(f32[4,32,8,544]{3,2,1,0:T(8,128)} %get-tuple-element.662) | copy-start | bytes 6684676 | tf_op jit(solution)/shard_map/while
  505.0 5.0 copy-start.20
  519.7 6.9 copy-start.41
  523.5 13.5 %copy-start.28 = (pred[32]{0:T(512)(128)(4,1)}, pred[32]{0:T(512)(128)(4,1)S(1)}, u32[]{:S(2)}) copy-start(pred[32]{0:T(512)(128)(4,1)S(1)} %iota_compare_fusion.6) | copy-start | bytes 100 | tf_op jit(solution)/shard_map/while
  524.4 12.6 %copy-start.18 = (bf16[32,4,128]{2,0,1:T(8,128)(2,1)}, bf16[32,4,128]{2,0,1:T(8,128)(2,1)S(1)}, u32[]{:S(2)}) copy-start(bf16[32,4,128]{2,0,1:T(8,128)(2,1)S(1)} %copy.300) | copy-start | bytes 98308 | tf_op jit(solution)/shard_map/while
  541.9 10.0 %copy-start.2 = (f32[4,32,8,544]{3,2,1,0:T(8,128)S(1)}, f32[4,32,8,544]{3,2,1,0:T(8,128)}, u32[]{:S(2)}) copy-start(f32[4,32,8,544]{3,2,1,0:T(8,128)} %get-tuple-element.662) | copy-start | bytes 6684676 | tf_op jit(solution)/shard_map/while
  567.0 5.0 copy-start.20
  585.8 119.2 %reduce-scatter.5.cloned.1.call-start = ((), (), s32[]{:S(2)}) async-start(), calls=%async_computation.5 | async-start | bytes 2621440 | tf_op jit(solution)/shard_map/reduce_scatter | solution.py:167
  590.9 28.5 %copy-start.12 = (f32[512,4,128]{2,1,0:T(4,128)S(1)}, f32[512,4,128]{2,1,0:T(4,128)}, u32[]{:S(2)}) copy-start(f32[512,4,128]{2,1,0:T(4,128)} %copy-done.11) | copy-start | bytes 3145732
  590.9 28.5 %copy-start.22 = (f32[512,4]{1,0:T(8,128)S(1)}, f32[512,4]{1,0:T(8,128)}, u32[]{:S(2)}) copy-start(f32[512,4]{1,0:T(8,128)} %copy-done.21) | copy-start | bytes 24580
  622.7 81.2 %copy-start.10 = (f32[1,1,512,512]{3,2,0,1:T(8,128)S(1)}, f32[1,1,512,512]{3,2,0,1:T(8,128)}, u32[]{:S(2)}) copy-start(f32[1,1,512,512]{3,2,0,1:T(8,128)} %copy-done.9) | copy-start | bytes 3145732
  622.7 81.2 %copy-start.34 = (f32[512]{0:T(512)S(1)}, f32[512]{0:T(512)}, u32[]{:S(2)}) copy-start(f32[512]{0:T(512)} %copy-done.33) | copy-start | bytes 6148
  (160 other events, 341.9 us)
Sparse Core Ops, SparseCore 0:
  9.8 35.3 all-gather.4
  47.6 33.4 all-gather.2
  585.9 32.0 reduce-scatter.2
  621.2 32.5 reduce-scatter.4
where the time goes:
time: 717 us; the launch traced here: 712 us
  other arithmetic  219 us (31%)
  local copies, waits for them, and re-layouts  218 us (30%)
  waiting for transfers between devices  93.9 us (13%)
  blocking collectives  78 us (11%)
  matrix products  69 us (10%)
  loops' own time  19.6 us (3%)
  between operations  14.1 us (2%)
    sub x8, other arithmetic, slot_pass(): grad_prob - row_total  80.1 us
    psum x1, blocking collectives, body(): q_grad_all, k_grad_all = lax.psum((q_gain_part, k_local), ('dp', 'branch'))  78 us
    dot_general x40, matrix products, product(): jnp.einsum(pattern, first_op, second_op, preferred_element_type=jnp.float32)  47.1 us
    all_gather x1, waiting for transfers between devices, body(): lax.all_gather(sent_keys, 'branch', axis=1, tiled=True)  35.9 us
    all_gather x1, waiting for transfers between devices, body(): lax.all_gather(prefix_values, 'branch', axis=1, tiled=True)  31.5 us
    slice x16, local copies, waits for them, and re-layouts, slot_pass(): grad_keys[:pre_len].reshape(pre_len, -1)  30 us
    dynamic_update_slice x16, local copies, waits for them, and re-layouts, step(): lax.dynamic_update_index_in_dim(acc_k, lax.dynamic_index_in_dim(acc_k, ow...  29.5 us
    reduce_scatter x1, waiting for transfers between devices, body(): lax.psum_scatter(part_k.astype(jnp.bfloat16), 'branch', scatter_dimension...  25.8 us
  transfers between devices with their start and end apart: 4, of which 3 were waited for; matrix products, arithmetic and copies ran while one was open for 3% of the time, Pallas kernels for 0%

commit v1 on v0

v1 whole, which is shorter than its diff:
```python
import functools
import math

import jax
import jax.numpy as jnp
from jax import lax
from jax.experimental import pallas as pl
from jax.experimental.pallas import tpu as pltpu
from jax.sharding import PartitionSpec as P

EPSILON = 1e-06
MESH = pl.DeviceIdType.MESH
F32 = jnp.float32
BF16 = jnp.bfloat16
LOG2E = math.log2(math.e)
LN2 = math.log(2.0)


def dot(a, b):
    return lax.dot_general(a, b, (((1,), (0,)), ((), ())), preferred_element_type=F32)


def dot_nt(a, b):
    return lax.dot_general(a, b, (((1,), (1,)), ((), ())), preferred_element_type=F32)


def norm_parts(raw):
    vals = raw.astype(F32)
    inv = lax.rsqrt(jnp.mean(vals * vals, axis=-1, keepdims=True) + EPSILON)
    return vals * inv, inv


def kernel(
    dims,
    pk, pv, q, rk, rv, g, q_gain, k_gain, lengths, prompts, owners,
    att, dq, d_rk, d_rv, d_pk, d_pv, qg_out, kg_out,
    qv, gv, attv, dqv, rkv, rvv, drkv, drvv, kraw,
    kb0, kb1, kb2, kb3, vb0, vb1, vb2, vb3,
    kt, vt, ck, cv, es, eb, ub, gq, gacc, rs_out, rs_in, dpk, dpv, ex1, ex2, ex3, meta,
    ag_send, ag_recv, rs_send, rs_recv, gx_send, gx_recv, load_sem, store_sem,
):
    n_dp, n_branch, inner, slots, rows, heads, group, pre, hd = dims
    outer = n_dp // inner
    kb, vb = (kb0, kb1, kb2, kb3), (vb0, vb1, vb2, vb3)
    width = group * hd
    cols = group * rows
    score_scale = 1.0 / math.sqrt(hd)

    me = lax.axis_index("branch")
    dp = lax.axis_index("dp")
    right = lax.rem(me + 1, n_branch)
    left = lax.rem(me + n_branch - 1, n_branch)
    in_c = lax.rem(dp, inner)
    out_c = dp // inner
    stages = (
        (ex1, me, n_branch, lambda k: {"branch": lax.rem(me + k, n_branch)}),
        (ex2, in_c, inner, lambda k: {"dp": out_c * inner + lax.rem(in_c + k, inner)}),
        (ex3, out_c, outer, lambda k: {"dp": lax.rem(out_c + k, outer) * inner + in_c}),
    )

    def head_cols(h):
        return pl.ds(h * hd, hd)

    k_loads = [
        pltpu.make_async_copy(pk.at[:, head_cols(h)], kraw.at[h], load_sem.at[h])
        for h in range(heads)
    ]
    v_loads = [
        pltpu.make_async_copy(pv.at[:, head_cols(h)], vb[h].at[0], load_sem.at[heads + h])
        for h in range(heads)
    ]
    base = 2 * heads
    rest_loads = [
        pltpu.make_async_copy(src, dst, load_sem.at[base + i])
        for i, (src, dst) in enumerate(((q, qv), (g, gv), (rk, rkv), (rv, rvv)))
    ]
    for h in range(heads):
        k_loads[h].start()
        v_loads[h].start()
    for copy in rest_loads:
        copy.start()

    barrier = pltpu.get_barrier_semaphore()
    partners = 0
    for _, _, extent, partner in stages:
        for k in range(1, extent):
            pl.semaphore_signal(barrier, inc=1, device_id=partner(k), device_id_type=MESH)
            partners += 1

    kg_row = k_gain[...]
    qg_row = q_gain[...]

    def own_hat(h):
        k_loads[h].wait()
        normed, _ = norm_parts(kraw[h])
        kb[h][0] = (normed * kg_row).astype(BF16)
        v_loads[h].wait()

    def remote(src, dst, send, recv, to):
        return pltpu.make_async_remote_copy(
            src_ref=src, dst_ref=dst, send_sem=send, recv_sem=recv,
            device_id={"branch": to}, device_id_type=MESH,
        )

    def ag(h, i):
        src, dst, to = (
            (kb[h].at[0], kb[h].at[3], right),
            (vb[h].at[0], vb[h].at[1], left),
            (vb[h].at[0], vb[h].at[3], right),
            (kb[h].at[0], kb[h].at[1], left),
            (kb[h].at[3], kb[h].at[2], right),
            (vb[h].at[1], vb[h].at[2], left),
        )[i]
        return remote(src, dst, ag_send.at[h, i], ag_recv.at[h, i], to)

    def ag_direct(h):
        for i in range(4):
            ag(h, i).start()

    def ag_forward(h):
        ag(h, 0).wait_recv()
        ag(h, 4).start()
        ag(h, 1).wait_recv()
        ag(h, 5).start()

    def ag_rest(h):
        for i in range(2, 6):
            ag(h, i).wait_recv()

    def rs(h, i):
        to = right if i % 2 == 0 else left
        return remote(rs_out.at[h, i], rs_in.at[h, i], rs_send.at[h, i], rs_recv.at[h, i], to)

    def rs_first(h):
        def part(acc, scale, r):
            return acc[meta[2, r]] * scale

        rs_out[h, 0] = part(ck, LN2, 2).astype(BF16)
        rs(h, 0).start()
        rs_out[h, 1] = part(cv, 1.0, 2).astype(BF16)
        rs(h, 1).start()
        rs_out[h, 2] = part(cv, 1.0, 1).astype(BF16)
        rs(h, 2).start()
        rs_out[h, 3] = part(ck, LN2, 3).astype(BF16)
        rs(h, 3).start()
        rs_out[h, 4] = part(ck, LN2, 1).astype(BF16)
        rs_out[h, 5] = part(cv, 1.0, 3).astype(BF16)

    def rs_second(h):
        for i in (0, 1):
            rs(h, i).wait_recv()
            rs_out[h, 4 + i] = (rs_out[h, 4 + i].astype(F32) + rs_in[h, i].astype(F32)).astype(BF16)
            rs(h, 4 + i).start()

    def out_copy(src, dst, i):
        return pltpu.make_async_copy(src, dst, store_sem.at[i])

    def prefix_out(h):
        return (
            out_copy(dpk.at[h], d_pk.at[:, head_cols(h)], 2 * heads + h),
            out_copy(dpv.at[h], d_pv.at[:, head_cols(h)], 3 * heads + h),
        )

    def rs_final(h):
        for i in range(2, 6):
            rs(h, i).wait_recv()
        grad = rs_in[h, 3].astype(F32) + rs_in[h, 4].astype(F32)
        normed, inv = norm_parts(kraw[h])
        scaled = grad * kg_row
        back = inv * (scaled - normed * jnp.mean(scaled * normed, axis=-1, keepdims=True))
        dpk[h] = back.astype(BF16)
        dpv[h] = (rs_in[h, 2].astype(F32) + rs_in[h, 5].astype(F32)).astype(BF16)
        for copy in prefix_out(h):
            copy.start()

    def head_out(h):
        part = pl.ds(h * width, width)
        return (
            out_copy(attv.at[:, :, part], att.at[:, :, part], h),
            out_copy(dqv.at[:, :, part], dq.at[:, :, part], heads + h),
        )

    def transposes(h):
        for r in range(1, n_branch):
            kt[r] = kb[h][r].T
            vt[r] = vb[h][r].T

    block = 128
    lane = lax.broadcasted_iota(jnp.int32, (1, cols), 1)
    token = lane & (rows - 1)

    def slot_pass(s, h, u):
        rel = meta[0, s]
        prev = meta[1, s]
        live = token < lengths[s]
        at = [h * width + i * hd for i in range(group)]
        q_t = jnp.concatenate([qv[s, :, a : a + hd] for a in at], axis=0).T.astype(F32)
        g_t = jnp.concatenate([gv[s, :, a : a + hd] for a in at], axis=0).T.astype(F32)
        g_t = jnp.where(live, g_t, 0.0)
        g_low = g_t.astype(BF16)
        q_inv = lax.rsqrt(jnp.mean(q_t * q_t, axis=0, keepdims=True) + EPSILON)
        q_n = q_t * q_inv
        gain = gq[...]
        q_scaled = q_n * (gain * (LOG2E * score_scale))
        q_low = q_scaled.astype(BF16)
        k_n, k_inv = norm_parts(rkv[s, :, h * hd : (h + 1) * hd])
        k_low = (k_n * kg_row).astype(BF16)
        v_low = rvv[s, :, h * hd : (h + 1) * hd]

        allowed = lax.broadcasted_iota(jnp.int32, (rows, cols), 0) <= token
        e_r = jnp.where(allowed, jnp.exp2(dot(k_low, q_low)), 0.0)
        total = jnp.sum(e_r, axis=0, keepdims=True)
        for c in range(pre // block):
            part = pl.ds(c * block, block)
            e_c = jnp.exp2(dot(kb[h][rel, part, :], q_low))
            es[u, part, :] = e_c
            eb[u, part, :] = e_c.astype(BF16)
            total += jnp.sum(e_c, axis=0, keepdims=True)
        inv = 1.0 / total
        e_r_low = e_r.astype(BF16)
        o_t = (dot(vt[rel], eb[u]) + dot(v_low.T, e_r_low)) * inv
        dots = jnp.sum(g_t * o_t, axis=0, keepdims=True)
        o_low = jnp.where(live, o_t, 0.0).astype(BF16).T
        for i, a in enumerate(at):
            attv[s, :, a : a + hd] = o_low[i * rows : (i + 1) * rows, :]

        u_r = (e_r * (dot(v_low, g_low) - dots)).astype(BF16)
        for c in range(pre // block):
            part = pl.ds(c * block, block)
            d_c = dot(vb[h][rel, part, :], g_low)
            ub[u, part, :] = (es[u, part, :] * (d_c - dots)).astype(BF16)
        dq_t = (dot(kt[rel], ub[u]) + dot(k_low.T, u_r)) * (inv * score_scale)
        gacc[...] += q_n * dq_t
        scaled = gain * dq_t
        back = q_inv * (scaled - q_n * jnp.mean(scaled * q_n, axis=0, keepdims=True))
        back_low = back.astype(BF16).T
        for i, a in enumerate(at):
            dqv[s, :, a : a + hd] = back_low[i * rows : (i + 1) * rows, :]

        q_part = (q_scaled * inv).astype(BF16)
        g_part = (g_t * inv).astype(BF16)
        dk_r = dot_nt(u_r, q_part) * LN2
        scaled_k = dk_r * kg_row
        back_k = k_inv * (scaled_k - k_n * jnp.mean(scaled_k * k_n, axis=-1, keepdims=True))
        drkv[s, :, h * hd : (h + 1) * hd] = back_k.astype(BF16)
        drvv[s, :, h * hd : (h + 1) * hd] = dot_nt(e_r_low, g_part).astype(BF16)
        for c in range(pre // block):
            part = pl.ds(c * block, block)
            ck[s, part, :] = ck[prev, part, :] + dot_nt(ub[u, part, :], q_part)
            cv[s, part, :] = cv[prev, part, :] + dot_nt(eb[u, part, :], g_part)

    def run_slots(h, first, count):
        def step(i, carry):
            for u in range(2):
                slot_pass(first + 2 * i + u, h, u)
            return carry

        lax.fori_loop(0, count // 2, step, 0)

    own_hat(0)
    pl.semaphore_wait(barrier, partners)
    ag_direct(0)
    own_hat(1)
    ag_forward(0)
    ag_direct(1)
    for h in range(2, heads):
        own_hat(h)

    rels = []
    for s in range(slots):
        rel = owners[prompts[s]] - me
        rel = jnp.where(rel < 0, rel + n_branch, rel)
        prev = jnp.int32(slots)
        for before in range(s):
            prev = jnp.where(rels[before] == rel, before, prev)
        rels.append(rel)
        meta[0, s] = rel
        meta[1, s] = prev
    for r in range(1, n_branch):
        last = jnp.int32(slots)
        for s in range(slots):
            last = jnp.where(rels[s] == r, s, last)
        meta[2, r] = last
    ck[slots] = jnp.zeros((pre, hd), F32)
    cv[slots] = jnp.zeros((pre, hd), F32)
    gq[...] = jnp.broadcast_to(qg_row, (cols, hd)).T
    gacc[...] = jnp.zeros_like(gacc)
    for copy in rest_loads:
        copy.wait()

    half = slots // 2
    for h in range(heads):
        ag_rest(h)
        transposes(h)
        run_slots(h, 0, half)
        if h + 1 < heads:
            ag_forward(h + 1)
        if h + 2 < heads:
            ag_direct(h + 2)
        if h >= 2:
            rs_second(h - 2)
        run_slots(h, half, slots - half)
        rs_first(h)
        for copy in head_out(h):
            copy.start()
        if h >= 3:
            rs_final(h - 3)
    resp_out = (out_copy(drkv, d_rk, 4 * heads), out_copy(drvv, d_rv, 4 * heads + 1))
    for copy in resp_out:
        copy.start()

    value = jnp.sum(gacc[...].T, axis=0, keepdims=True)

    def exchange(i, value):
        buf, place, extent, partner = stages[i]
        buf[place] = jnp.broadcast_to(value, (8, hd))
        for k in range(1, extent):
            gain_copy(i, k).start()

    def gain_copy(i, k):
        buf, place, _, partner = stages[i]
        return pltpu.make_async_remote_copy(
            src_ref=buf.at[place], dst_ref=buf.at[place],
            send_sem=gx_send.at[i, k], recv_sem=gx_recv.at[i, k],
            device_id=partner(k), device_id_type=MESH,
        )

    def collect(i):
        buf, _, extent, _ = stages[i]
        for k in range(1, extent):
            gain_copy(i, k).wait_recv()
        value = buf[0]
        for k in range(1, extent):
            value = value + buf[k]
        return value[0:1, :]

    exchange(0, value)
    rs_second(heads - 2)
    exchange(1, collect(0))
    rs_second(heads - 1)
    rs_final(heads - 3)
    exchange(2, collect(1))
    rs_final(heads - 2)
    value = collect(2)
    qg_out[...] = value
    kg_out[...] = value * qg_row / kg_row
    rs_final(heads - 1)

    for h in range(heads):
        for i in range(6):
            ag(h, i).wait_send()
            rs(h, i).wait_send()
    for i, (_, _, extent, _) in enumerate(stages):
        for k in range(1, extent):
            gain_copy(i, k).wait_send()
    for h in range(heads):
        for copy in head_out(h) + prefix_out(h):
            copy.wait()
    for copy in resp_out:
        copy.wait()


def body(
    n_dp, n_branch,
    prefix_keys, prefix_values, resp_query, resp_keys, resp_values, out_grad,
    q_gain, k_gain, lengths, slot_prompt, prefix_owner,
):
    hd = q_gain.shape[0]
    pre, kvw = prefix_keys.shape[2:]
    slots, rows, qw = resp_query.shape[2:]
    heads = kvw // hd
    group = qw // kvw
    inner = math.gcd(n_dp, 8)
    outer = n_dp // inner
    cols = group * rows
    hbm = pl.BlockSpec(memory_space=pl.ANY)
    vmem = pl.BlockSpec(memory_space=pltpu.VMEM)
    smem = pl.BlockSpec(memory_space=pltpu.SMEM)

    def held(dtype, *shape):
        return pltpu.VMEM(shape, dtype)

    prefix_slots = [held(BF16, n_branch, pre, hd) for _ in range(2 * heads)]
    outs = pl.pallas_call(
        functools.partial(kernel, (n_dp, n_branch, inner, slots, rows, heads, group, pre, hd)),
        out_shape=(
            jax.ShapeDtypeStruct((slots, rows, qw), BF16),
            jax.ShapeDtypeStruct((slots, rows, qw), BF16),
            jax.ShapeDtypeStruct((slots, rows, kvw), BF16),
            jax.ShapeDtypeStruct((slots, rows, kvw), BF16),
            jax.ShapeDtypeStruct((pre, kvw), BF16),
            jax.ShapeDtypeStruct((pre, kvw), BF16),
            jax.ShapeDtypeStruct((1, hd), F32),
            jax.ShapeDtypeStruct((1, hd), F32),
        ),
        in_specs=[hbm] * 6 + [vmem] * 2 + [smem] * 3,
        out_specs=(hbm,) * 6 + (vmem,) * 2,
        scratch_shapes=[
            held(BF16, slots, rows, qw),
            held(BF16, slots, rows, qw),
            held(BF16, slots, rows, qw),
            held(BF16, slots, rows, qw),
            held(BF16, slots, rows, kvw),
            held(BF16, slots, rows, kvw),
            held(BF16, slots, rows, kvw),
            held(BF16, slots, rows, kvw),
            held(BF16, heads, pre, hd),
            *prefix_slots,
            held(BF16, n_branch, hd, pre),
            held(BF16, n_branch, hd, pre),
            held(F32, slots + 1, pre, hd),
            held(F32, slots + 1, pre, hd),
            held(F32, 2, pre, cols),
            held(BF16, 2, pre, cols),
            held(BF16, 2, pre, cols),
            held(F32, hd, cols),
            held(F32, hd, cols),
            held(BF16, heads, 6, pre, hd),
            held(BF16, heads, 6, pre, hd),
            held(BF16, heads, pre, hd),
            held(BF16, heads, pre, hd),
            held(F32, n_branch, 8, hd),
            held(F32, inner, 8, hd),
            held(F32, outer, 8, hd),
            pltpu.SMEM((3, slots), jnp.int32),
            pltpu.SemaphoreType.DMA((heads, 6)),
            pltpu.SemaphoreType.DMA((heads, 6)),
            pltpu.SemaphoreType.DMA((heads, 6)),
            pltpu.SemaphoreType.DMA((heads, 6)),
            pltpu.SemaphoreType.DMA((3, 8)),
            pltpu.SemaphoreType.DMA((3, 8)),
            pltpu.SemaphoreType.DMA((2 * heads + 4,)),
            pltpu.SemaphoreType.DMA((4 * heads + 2,)),
        ],
        compiler_params=pltpu.CompilerParams(
            collective_id=0, has_side_effects=True, vmem_limit_bytes=56 * 1024 * 1024
        ),
    )(
        prefix_keys[0, 0], prefix_values[0, 0], resp_query[0, 0], resp_keys[0, 0],
        resp_values[0, 0], out_grad[0, 0], q_gain[None], k_gain[None],
        lengths[0, 0], slot_prompt[0, 0], prefix_owner[0],
    )
    return tuple(x[None, None] for x in outs[:6]) + (outs[6][0], outs[7][0])


def solution(mesh):
    block = P("dp", "branch")
    return jax.shard_map(
        functools.partial(body, mesh.shape["dp"], mesh.shape["branch"]),
        mesh=mesh,
        in_specs=(block,) * 6 + (P(), P()) + (block, block, P("dp")),
        out_specs=(block,) * 6 + (P(), P()),
        check_vma=False,
    )
```

time: 717 us -> 97.6 us (0.14)
  other arithmetic: 219 us -> 0 us
  local copies, waits for them, and re-layouts: 218 us -> 8.64 us
  waiting for transfers between devices: 93.9 us -> 0 us
  Pallas kernels: 0 us -> 87.1 us
  blocking collectives: 78 us -> 0 us
  matrix products: 69 us -> 0 us
  loops' own time: 19.6 us -> 0 us
  between operations: 14.1 us -> 0.67 us
    pallas_call x0 -> x1, Pallas kernels: none -> 87.1 us  [body(): pl.pallas_call(functools.partial(kernel, (n_dp, n_branch, inner, slots, r...]
    sub x16 -> x0, other arithmetic: 80.2 us -> none  [the longest x8 80.1 us: slot_pass(): grad_prob - row_total]
    psum x1 -> x0, blocking collectives: 78 us -> none  [body(): q_grad_all, k_grad_all = lax.psum((q_gain_part, k_local), ('dp', 'branch'))]
    all_gather x2 -> x0, waiting for transfers between devices: 67.4 us -> none  [the longest x1 35.9 us: body(): lax.all_gather(sent_keys, 'branch', axis=1, tiled=True)]
    dynamic_update_slice x48 -> x0, local copies, waits for them, and re-layouts: 50.6 us -> none  [the longest x16 29.5 us: step(): lax.dynamic_update_index_in_dim(acc_k, lax.dynamic_index_in_dim(acc_k, ow...]
    dynamic_slice x64 -> x0, local copies, waits for them, and re-layouts: 49.7 us -> none  [the longest x16 16.3 us: step(): lax.dynamic_index_in_dim(acc_v, owner, 0, keepdims=False) + results[5]]
    dot_general x40 -> x0, matrix products: 47.1 us -> none  [product(): jnp.einsum(pattern, first_op, second_op, preferred_element_type=jnp.float32)]
    convert_element_type x44 -> x0, other arithmetic: 40.1 us -> none  [the longest x8 12.6 us: slot_pass(): grad_k.reshape(resp_len, -1).astype(jnp.bfloat16)]
  transfers between devices with their start and end apart: 4 -> 0, of which waited for: 3 -> 0; matrix products, arithmetic and copies ran while one was open for 3% -> 0% of each run, Pallas kernels for 0% -> 0%
where the time goes in v1:
time: 97.6 us; the launch traced here: 96.4 us
  Pallas kernels  87.1 us (89%)
  local copies, waits for them, and re-layouts  8.64 us (9%)
    pallas_call x1, Pallas kernels, body(): pl.pallas_call(functools.partial(kernel, (n_dp, n_branch, inner, slots, r...  87.1 us
    unnamed x22, local copies, waits for them, and re-layouts  8.64 us

profile of v1, /device:TPU:8, one launch (start us, length us, event | category | flops | bytes accessed | tf_op | source)
XLA Modules:
  0.0 96.4 jit_solution(18363283338403989685)
XLA Ops:
  0.6 87.1 %shard_map.170 = (bf16[8,32,4096]{2,1,0:T(8,128)(2,1)}, bf16[8,32,4096]{2,1,0:T(8,128)(2,1)}, bf16[8,32,512]{2,1,0:T(8,128)(2,1)}, bf16[8,32,512]{2,1,0:T(8,128)...) custom-call(bf16[512,512]{1,0:T(8,128)(2,1)} %bitcast.25, ...), custom_call_target="tpu_custom_call" | custom-call | tf_op jit(solution)/shard_map/pallas_call | solution.py:384
  87.8 0.0 copy-start
  87.8 3.3 %copy.27 = bf16[1,1,8,32,4096]{4,3,2,1,0:T(8,128)(2,1)} copy(bf16[1,1,8,32,4096]{4,3,2,1,0:T(8,128)(2,1)} %bitcast.22) | data formatting | bytes 4194304
  91.0 0.0 copy-done
  91.0 0.0 copy-start.4
  91.1 0.0 copy-start.3
  91.1 0.0 copy-start.2
  91.1 1.3 %copy.28 = bf16[1,1,8,32,4096]{4,3,2,1,0:T(8,128)(2,1)} copy(bf16[1,1,8,32,4096]{4,3,2,1,0:T(8,128)(2,1)S(1)} %bitcast.21) | data formatting | bytes 4194304
  92.4 0.0 copy-done.4
  92.4 0.0 copy-start.1
  92.4 0.0 copy-start.6
  92.4 0.0 copy-start.5
  92.4 0.7 copy.29
  93.1 0.0 copy-done.3
  93.1 0.7 copy.30
  93.8 0.0 copy-done.2
  93.8 0.8 copy.31
  94.6 0.0 copy-done.1
  94.6 0.8 copy.32
  95.4 0.0 copy-done.6
  95.4 0.5 copy.33
  95.9 0.0 copy-done.5
  95.9 0.5 copy.34
Async XLA Ops:
  87.8 3.3 %copy-start = (bf16[8,32,4096]{2,1,0:T(8,128)(2,1)S(1)}, bf16[8,32,4096]{2,1,0:T(8,128)(2,1)}, u32[]{:S(2)}) copy-start(bf16[8,32,4096]{2,1,0:T(8,128)(2,1)} %get-tuple-element.17) | copy-start | bytes 6291460
  91.0 1.3 %copy-start.4 = (bf16[8,32,512]{2,1,0:T(8,128)(2,1)S(1)}, bf16[8,32,512]{2,1,0:T(8,128)(2,1)}, u32[]{:S(2)}) copy-start(bf16[8,32,512]{2,1,0:T(8,128)(2,1)} %get-tuple-element.18) | copy-start | bytes 786436
  91.1 2.0 %copy-start.3 = (bf16[8,32,512]{2,1,0:T(8,128)(2,1)S(1)}, bf16[8,32,512]{2,1,0:T(8,128)(2,1)}, u32[]{:S(2)}) copy-start(bf16[8,32,512]{2,1,0:T(8,128)(2,1)} %get-tuple-element.19) | copy-start | bytes 786436
  91.1 2.8 %copy-start.2 = (bf16[512,512]{1,0:T(8,128)(2,1)S(1)}, bf16[512,512]{1,0:T(8,128)(2,1)}, u32[]{:S(2)}) copy-start(bf16[512,512]{1,0:T(8,128)(2,1)} %get-tuple-element.20) | copy-start | bytes 1572868
  92.4 2.2 %copy-start.1 = (bf16[512,512]{1,0:T(8,128)(2,1)S(1)}, bf16[512,512]{1,0:T(8,128)(2,1)}, u32[]{:S(2)}) copy-start(bf16[512,512]{1,0:T(8,128)(2,1)} %get-tuple-element.21) | copy-start | bytes 1572868
  92.4 3.0 %copy-start.6 = (f32[1,128]{1,0:T(1,128)S(1)}, f32[1,128]{1,0:T(1,128)}, u32[]{:S(2)}) copy-start(f32[1,128]{1,0:T(1,128)} %get-tuple-element.22) | copy-start | bytes 1540
  92.4 3.5 %copy-start.5 = (f32[1,128]{1,0:T(1,128)S(1)}, f32[1,128]{1,0:T(1,128)}, u32[]{:S(2)}) copy-start(f32[1,128]{1,0:T(1,128)} %get-tuple-element.23) | copy-start | bytes 1540

commit v2 on v1

--- a/solution.py
+++ b/solution.py
@@ -33,11 +33,11 @@
 def kernel(
     dims,
     pk, pv, q, rk, rv, g, q_gain, k_gain, lengths, prompts, owners,
-    att, dq, d_rk, d_rv, d_pk, d_pv, qg_out, kg_out,
-    qv, gv, attv, dqv, rkv, rvv, drkv, drvv, kraw,
+    attv, dqv, drkv, drvv, dpk, dpv, qg_out, kg_out,
+    qv, gv, rkv, rvv, kraw,
     kb0, kb1, kb2, kb3, vb0, vb1, vb2, vb3,
-    kt, vt, ck, cv, es, eb, ub, gq, gacc, rs_out, rs_in, dpk, dpv, ex1, ex2, ex3, meta,
-    ag_send, ag_recv, rs_send, rs_recv, gx_send, gx_recv, load_sem, store_sem,
+    kt, vt, ck, cv, es, eb, ub, gq, gacc, rs_out, rs_in, ex1, ex2, ex3, ex4, meta,
+    ag_send, ag_recv, rs_send, rs_recv, gx_send, gx_recv, load_sem, ready,
 ):
     n_dp, n_branch, inner, slots, rows, heads, group, pre, hd = dims
     outer = n_dp // inner
@@ -53,10 +53,47 @@
     in_c = lax.rem(dp, inner)
     out_c = dp // inner
     stages = (
-        (ex1, me, n_branch, lambda k: {"branch": lax.rem(me + k, n_branch)}),
         (ex2, in_c, inner, lambda k: {"dp": out_c * inner + lax.rem(in_c + k, inner)}),
         (ex3, out_c, outer, lambda k: {"dp": lax.rem(out_c + k, outer) * inner + in_c}),
     )
+    met = inner + outer - 2
+
+    barrier = pltpu.get_barrier_semaphore()
+
+    def tell(sem, to):
+        pl.semaphore_signal(sem, inc=1, device_id=to, device_id_type=MESH)
+
+    @pl.when(me == 2)
+    def _():
+        tell(barrier, {"branch": 1})
+        tell(barrier, {"branch": 3})
+
+    @pl.when((me == 1) | (me == 3))
+    def _():
+        tell(barrier, {"branch": 2})
+
+    @pl.when(me == 0)
+    def _():
+        for k in (1, 3, 2):
+            tell(barrier, {"branch": k})
+        for _, _, extent, partner in stages:
+            for k in range(1, extent):
+                tell(barrier, partner(k))
+
+    def enter():
+        @pl.when(me == 2)
+        def _():
+            pl.semaphore_wait(barrier, 3)
+            tell(ready.at[1], {"branch": 0})
+
+        @pl.when((me == 1) | (me == 3))
+        def _():
+            pl.semaphore_wait(barrier, 2)
+            tell(ready.at[0], {"branch": 0})
+
+        @pl.when(me == 0)
+        def _():
+            pl.semaphore_wait(ready.at[0], 2)
 
     def head_cols(h):
         return pl.ds(h * hd, hd)
@@ -80,13 +117,6 @@
     for copy in rest_loads:
         copy.start()
 
-    barrier = pltpu.get_barrier_semaphore()
-    partners = 0
-    for _, _, extent, partner in stages:
-        for k in range(1, extent):
-            pl.semaphore_signal(barrier, inc=1, device_id=partner(k), device_id_type=MESH)
-            partners += 1
-
     kg_row = k_gain[...]
     qg_row = q_gain[...]
 
@@ -152,15 +182,6 @@
             rs_out[h, 4 + i] = (rs_out[h, 4 + i].astype(F32) + rs_in[h, i].astype(F32)).astype(BF16)
             rs(h, 4 + i).start()
 
-    def out_copy(src, dst, i):
-        return pltpu.make_async_copy(src, dst, store_sem.at[i])
-
-    def prefix_out(h):
-        return (
-            out_copy(dpk.at[h], d_pk.at[:, head_cols(h)], 2 * heads + h),
-            out_copy(dpv.at[h], d_pv.at[:, head_cols(h)], 3 * heads + h),
-        )
-
     def rs_final(h):
         for i in range(2, 6):
             rs(h, i).wait_recv()
@@ -168,17 +189,8 @@
         normed, inv = norm_parts(kraw[h])
         scaled = grad * kg_row
         back = inv * (scaled - normed * jnp.mean(scaled * normed, axis=-1, keepdims=True))
-        dpk[h] = back.astype(BF16)
-        dpv[h] = (rs_in[h, 2].astype(F32) + rs_in[h, 5].astype(F32)).astype(BF16)
-        for copy in prefix_out(h):
-            copy.start()
-
-    def head_out(h):
-        part = pl.ds(h * width, width)
-        return (
-            out_copy(attv.at[:, :, part], att.at[:, :, part], h),
-            out_copy(dqv.at[:, :, part], dq.at[:, :, part], heads + h),
-        )
+        dpk[:, h * hd : (h + 1) * hd] = back.astype(BF16)
+        dpv[:, h * hd : (h + 1) * hd] = (rs_in[h, 2].astype(F32) + rs_in[h, 5].astype(F32)).astype(BF16)
 
     def transposes(h):
         for r in range(1, n_branch):
@@ -258,7 +270,7 @@
         lax.fori_loop(0, count // 2, step, 0)
 
     own_hat(0)
-    pl.semaphore_wait(barrier, partners)
+    enter()
     ag_direct(0)
     own_hat(1)
     ag_forward(0)
@@ -300,63 +312,114 @@
         if h >= 2:
             rs_second(h - 2)
         run_slots(h, half, slots - half)
-        rs_first(h)
-        for copy in head_out(h):
-            copy.start()
+        if h + 1 < heads:
+            rs_first(h)
         if h >= 3:
             rs_final(h - 3)
-    resp_out = (out_copy(drkv, d_rk, 4 * heads), out_copy(drvv, d_rv, 4 * heads + 1))
-    for copy in resp_out:
-        copy.start()
-
-    value = jnp.sum(gacc[...].T, axis=0, keepdims=True)
-
-    def exchange(i, value):
-        buf, place, extent, partner = stages[i]
-        buf[place] = jnp.broadcast_to(value, (8, hd))
-        for k in range(1, extent):
-            gain_copy(i, k).start()
-
-    def gain_copy(i, k):
+
+    def spread(value):
+        return jnp.broadcast_to(value, (8, hd))
+
+    ex1[me] = spread(jnp.sum(gacc[...].T, axis=0, keepdims=True))
+
+    def gain_copy(src, dst, i, k, j, to):
+        return pltpu.make_async_remote_copy(
+            src_ref=src, dst_ref=dst, send_sem=gx_send.at[i, k], recv_sem=gx_recv.at[i, j],
+            device_id=to, device_id_type=MESH,
+        )
+
+    def up(place):
+        return gain_copy(ex1.at[place], ex1.at[place], 0, 0, place, {"branch": 0})
+
+    def down(k):
+        return gain_copy(ex4, ex4, 3, k, 0, {"branch": k})
+
+    def across(i, k):
         buf, place, _, partner = stages[i]
-        return pltpu.make_async_remote_copy(
-            src_ref=buf.at[place], dst_ref=buf.at[place],
-            send_sem=gx_send.at[i, k], recv_sem=gx_recv.at[i, k],
-            device_id=partner(k), device_id_type=MESH,
-        )
-
-    def collect(i):
-        buf, _, extent, _ = stages[i]
-        for k in range(1, extent):
-            gain_copy(i, k).wait_recv()
+        return gain_copy(buf.at[place], buf.at[place], 1 + i, k, k, partner(k))
+
+    def collect(buf, extent, copies):
+        for copy in copies:
+            copy.wait_recv()
         value = buf[0]
         for k in range(1, extent):
             value = value + buf[k]
-        return value[0:1, :]
-
-    exchange(0, value)
+        return value
+
+    def send_across(i, value):
+        buf, place, extent, _ = stages[i]
+        buf[place] = value
+        for k in range(1, extent):
+            across(i, k).start()
+
+    def collect_across(i):
+        buf, _, extent, _ = stages[i]
+        return collect(buf, extent, [across(i, k) for k in range(1, extent)])
+
+    @pl.when(me != 0)
+    def _():
+        up(me).start()
+
+    rs_first(heads - 1)
     rs_second(heads - 2)
-    exchange(1, collect(0))
+
+    @pl.when(me == 0)
+    def _():
+        value = collect(ex1, n_branch, [up(k) for k in range(1, n_branch)])
+        pl.semaphore_wait(barrier, met)
+        send_across(0, value)
+
     rs_second(heads - 1)
     rs_final(heads - 3)
-    exchange(2, collect(1))
+
+    @pl.when(me == 0)
+    def _():
+        send_across(1, collect_across(0))
+
     rs_final(heads - 2)
-    value = collect(2)
+
+    @pl.when(me == 0)
+    def _():
+        ex4[...] = collect_across(1)
+        pl.semaphore_wait(ready.at[1], 1)
+        for k in range(1, n_branch):
+            down(k).start()
+
+    rs_final(heads - 1)
+
+    @pl.when(me != 0)
+    def _():
+        down(me).wait_recv()
+
+    value = ex4[0:1, :]
     qg_out[...] = value
     kg_out[...] = value * qg_row / kg_row
-    rs_final(heads - 1)
 
     for h in range(heads):
         for i in range(6):
             ag(h, i).wait_send()
             rs(h, i).wait_send()
-    for i, (_, _, extent, _) in enumerate(stages):
-        for k in range(1, extent):
-            gain_copy(i, k).wait_send()
-    for h in range(heads):
-        for copy in head_out(h) + prefix_out(h):
-            copy.wait()
-    for copy in resp_out:
+
+    @pl.when(me != 0)
+    def _():
+        up(me).wait_send()
+
+    @pl.when(me == 0)
+    def _():
+        for i, (_, _, extent, _) in enumerate(stages):
+            for k in range(1, extent):
+                across(i, k).wait_send()
+        for k in range(1, n_branch):
+            down(k).wait_send()
+
+
+def write_out(*refs):
+    count = len(refs) // 2
+    held, outs, sems = refs[:count], refs[count:-1], refs[-1]
+    copies = [pltpu.make_async_copy(a, b, sems.at[i]) for i, (a, b) in enumerate(zip(held, outs))]
+    for copy in copies:
+        copy.start()
+    for copy in copies:
         copy.wait()
 
 
@@ -373,7 +436,7 @@
     inner = math.gcd(n_dp, 8)
     outer = n_dp // inner
     cols = group * rows
-    hbm = pl.BlockSpec(memory_space=pl.ANY)
+    hbm = pl.BlockSpec(memory_space=pltpu.HBM)
     vmem = pl.BlockSpec(memory_space=pltpu.VMEM)
     smem = pl.BlockSpec(memory_space=pltpu.SMEM)
 
@@ -381,27 +444,24 @@
         return pltpu.VMEM(shape, dtype)
 
     prefix_slots = [held(BF16, n_branch, pre, hd) for _ in range(2 * heads)]
-    outs = pl.pallas_call(
+    shapes = (
+        ((slots, rows, qw), BF16),
+        ((slots, rows, qw), BF16),
+        ((slots, rows, kvw), BF16),
+        ((slots, rows, kvw), BF16),
+        ((pre, kvw), BF16),
+        ((pre, kvw), BF16),
+        ((1, hd), F32),
+        ((1, hd), F32),
+    )
+    results = pl.pallas_call(
         functools.partial(kernel, (n_dp, n_branch, inner, slots, rows, heads, group, pre, hd)),
-        out_shape=(
-            jax.ShapeDtypeStruct((slots, rows, qw), BF16),
-            jax.ShapeDtypeStruct((slots, rows, qw), BF16),
-            jax.ShapeDtypeStruct((slots, rows, kvw), BF16),
-            jax.ShapeDtypeStruct((slots, rows, kvw), BF16),
-            jax.ShapeDtypeStruct((pre, kvw), BF16),
-            jax.ShapeDtypeStruct((pre, kvw), BF16),
-            jax.ShapeDtypeStruct((1, hd), F32),
-            jax.ShapeDtypeStruct((1, hd), F32),
-        ),
+        out_shape=tuple(pltpu.VMEM(*x) for x in shapes),
         in_specs=[hbm] * 6 + [vmem] * 2 + [smem] * 3,
-        out_specs=(hbm,) * 6 + (vmem,) * 2,
+        out_specs=(vmem,) * 8,
         scratch_shapes=[
             held(BF16, slots, rows, qw),
             held(BF16, slots, rows, qw),
-            held(BF16, slots, rows, qw),
-            held(BF16, slots, rows, qw),
-            held(BF16, slots, rows, kvw),
-            held(BF16, slots, rows, kvw),
             held(BF16, slots, rows, kvw),
             held(BF16, slots, rows, kvw),
             held(BF16, heads, pre, hd),
@@ -417,29 +477,36 @@
             held(F32, hd, cols),
             held(BF16, heads, 6, pre, hd),
             held(BF16, heads, 6, pre, hd),
-            held(BF16, heads, pre, hd),
-            held(BF16, heads, pre, hd),
             held(F32, n_branch, 8, hd),
             held(F32, inner, 8, hd),
             held(F32, outer, 8, hd),
+            held(F32, 8, hd),
             pltpu.SMEM((3, slots), jnp.int32),
             pltpu.SemaphoreType.DMA((heads, 6)),
             pltpu.SemaphoreType.DMA((heads, 6)),
             pltpu.SemaphoreType.DMA((heads, 6)),
             pltpu.SemaphoreType.DMA((heads, 6)),
-            pltpu.SemaphoreType.DMA((3, 8)),
-            pltpu.SemaphoreType.DMA((3, 8)),
+            pltpu.SemaphoreType.DMA((4, 8)),
+            pltpu.SemaphoreType.DMA((4, 8)),
             pltpu.SemaphoreType.DMA((2 * heads + 4,)),
-            pltpu.SemaphoreType.DMA((4 * heads + 2,)),
+            pltpu.SemaphoreType.REGULAR((2,)),
         ],
         compiler_params=pltpu.CompilerParams(
-            collective_id=0, has_side_effects=True, vmem_limit_bytes=56 * 1024 * 1024
+            collective_id=0, has_side_effects=True, vmem_limit_bytes=int(58 * 1024 * 1024)
         ),
     )(
         prefix_keys[0, 0], prefix_values[0, 0], resp_query[0, 0], resp_keys[0, 0],
         resp_values[0, 0], out_grad[0, 0], q_gain[None], k_gain[None],
         lengths[0, 0], slot_prompt[0, 0], prefix_owner[0],
     )
+    outs = pl.pallas_call(
+        write_out,
+        out_shape=tuple(jax.ShapeDtypeStruct(*x) for x in shapes),
+        in_specs=[vmem] * 8,
+        out_specs=(hbm,) * 8,
+        scratch_shapes=[pltpu.SemaphoreType.DMA((8,))],
+        compiler_params=pltpu.CompilerParams(vmem_limit_bytes=4 * 1024 * 1024),
+    )(*results)
     return tuple(x[None, None] for x in outs[:6]) + (outs[6][0], outs[7][0])
 
 

time: 97.6 us -> 86.6 us (0.89); the launches traced: 96.4 us -> 86.5 us
  local copies, waits for them, and re-layouts: 8.64 us -> 0 us
  Pallas kernels: 87.1 us -> 85.7 us
    unnamed x22 -> x0, local copies, waits for them, and re-layouts: 8.64 us -> none
    pallas_call x1, Pallas kernels: 87.1 us -> 83.2 us  [body(): pl.pallas_call(functools.partial(kernel, (n_dp, n_branch, inner, slots, r...]
    pallas_call x0 -> x1, Pallas kernels: none -> 2.57 us  [body(): pl.pallas_call(write_out, out_shape=tuple((jax.ShapeDtypeStruct(*x) for x...]
where the time goes in v2:
time: 86.6 us; the launch traced here: 86.5 us
  Pallas kernels  85.7 us (99%)
    pallas_call x1, Pallas kernels, body(): pl.pallas_call(functools.partial(kernel, (n_dp, n_branch, inner, slots, r...  83.2 us
    pallas_call x1, Pallas kernels, body(): pl.pallas_call(write_out, out_shape=tuple((jax.ShapeDtypeStruct(*x) for x...  2.57 us

profile of v2, /device:TPU:8, one launch (start us, length us, event | category | flops | bytes accessed | tf_op | source)
XLA Modules:
  0.0 86.5 jit_solution(7955061347918159389)
XLA Ops:
  0.6 83.2 %shard_map.170 = (bf16[8,32,4096]{2,1,0:T(8,128)(2,1)S(1)}, bf16[8,32,4096]{2,1,0:T(8,128)(2,1)S(1)}, bf16[8,32,512]{2,1,0:T(8,128)(2,1)S(1)}, bf16[8,32,512]{2,...) custom-call(bf16[512,512]{1,0:T(8,128)(2,1)} %bitcast.21, ...), custom_call_target="tpu_custom_call" | custom-call | tf_op jit(solution)/shard_map/pallas_call | solution.py:457
  83.8 2.6 %shard_map.171 = (bf16[8,32,4096]{2,1,0:T(8,128)(2,1)}, bf16[8,32,4096]{2,1,0:T(8,128)(2,1)}, bf16[8,32,512]{2,1,0:T(8,128)(2,1)}, bf16[8,32,512]{2,1,0:T(8,128)...) custom-call(bf16[8,32,4096]{2,1,0:T(8,128)(2,1)S(1)} %get-tuple-element.24.ref, ...), custom_call_target="tpu_custom_call" | custom-call | tf_op jit(solution)/shard_map/pallas_call | solution.py:502

commit v3 on v2

--- a/solution.py
+++ b/solution.py
@@ -161,20 +161,15 @@
         to = right if i % 2 == 0 else left
         return remote(rs_out.at[h, i], rs_in.at[h, i], rs_send.at[h, i], rs_recv.at[h, i], to)
 
-    def rs_first(h):
-        def part(acc, scale, r):
-            return acc[meta[2, r]] * scale
-
-        rs_out[h, 0] = part(ck, LN2, 2).astype(BF16)
-        rs(h, 0).start()
-        rs_out[h, 1] = part(cv, 1.0, 2).astype(BF16)
-        rs(h, 1).start()
-        rs_out[h, 2] = part(cv, 1.0, 1).astype(BF16)
-        rs(h, 2).start()
-        rs_out[h, 3] = part(ck, LN2, 3).astype(BF16)
-        rs(h, 3).start()
-        rs_out[h, 4] = part(ck, LN2, 1).astype(BF16)
-        rs_out[h, 5] = part(cv, 1.0, 3).astype(BF16)
+    def rs_pack(h):
+        for i, (acc, scale, r) in enumerate(
+            ((ck, LN2, 2), (cv, 1.0, 2), (cv, 1.0, 1), (ck, LN2, 3), (ck, LN2, 1), (cv, 1.0, 3))
+        ):
+            rs_out[h, i] = (acc[meta[2, r]] * scale).astype(BF16)
+
+    def rs_start(h):
+        for i in range(4):
+            rs(h, i).start()
 
     def rs_second(h):
         for i in (0, 1):
@@ -261,13 +256,15 @@
             ck[s, part, :] = ck[prev, part, :] + dot_nt(ub[u, part, :], q_part)
             cv[s, part, :] = cv[prev, part, :] + dot_nt(eb[u, part, :], g_part)
 
-    def run_slots(h, first, count):
+    def run_head(h, events):
         def step(i, carry):
+            for at, event in events:
+                pl.when(i == at)(event)
             for u in range(2):
-                slot_pass(first + 2 * i + u, h, u)
+                slot_pass(2 * i + u, h, u)
             return carry
 
-        lax.fori_loop(0, count // 2, step, 0)
+        lax.fori_loop(0, slots // 2, step, 0)
 
     own_hat(0)
     enter()
@@ -300,22 +297,24 @@
     for copy in rest_loads:
         copy.wait()
 
-    half = slots // 2
+    def gather_next(h):
+        ag_forward(h)
+        if h + 1 < heads:
+            ag_direct(h + 1)
+        else:
+            for done in range(h - 1):
+                rs_start(done)
+
     for h in range(heads):
         ag_rest(h)
         transposes(h)
-        run_slots(h, 0, half)
         if h + 1 < heads:
-            ag_forward(h + 1)
-        if h + 2 < heads:
-            ag_direct(h + 2)
-        if h >= 2:
-            rs_second(h - 2)
-        run_slots(h, half, slots - half)
+            events = [(1, functools.partial(gather_next, h + 1))]
+        else:
+            events = [(2, functools.partial(rs_second, 0))]
+        run_head(h, events)
         if h + 1 < heads:
-            rs_first(h)
-        if h >= 3:
-            rs_final(h - 3)
+            rs_pack(h)
 
     def spread(value):
         return jnp.broadcast_to(value, (8, hd))
@@ -360,8 +359,10 @@
     def _():
         up(me).start()
 
-    rs_first(heads - 1)
-    rs_second(heads - 2)
+    rs_second(heads - 3)
+    rs_start(heads - 2)
+    rs_pack(heads - 1)
+    rs_start(heads - 1)
 
     @pl.when(me == 0)
     def _():
@@ -369,14 +370,15 @@
         pl.semaphore_wait(barrier, met)
         send_across(0, value)
 
+    rs_final(heads - 4)
+    rs_second(heads - 2)
+
+    @pl.when(me == 0)
+    def _():
+        send_across(1, collect_across(0))
+
+    rs_final(heads - 3)
     rs_second(heads - 1)
-    rs_final(heads - 3)
-
-    @pl.when(me == 0)
-    def _():
-        send_across(1, collect_across(0))
-
-    rs_final(heads - 2)
 
     @pl.when(me == 0)
     def _():
@@ -385,6 +387,7 @@
         for k in range(1, n_branch):
             down(k).start()
 
+    rs_final(heads - 2)
     rs_final(heads - 1)
 
     @pl.when(me != 0)

time: 86.6 us -> 78.7 us (0.909)
  Pallas kernels: 85.7 us -> 77.9 us
    pallas_call x1, Pallas kernels: 83.2 us -> 75.4 us  [body(): pl.pallas_call(functools.partial(kernel, (n_dp, n_branch, inner, slots, r...]
where the time goes in v3:
time: 78.7 us; the launch traced here: 78.6 us
  Pallas kernels  77.9 us (99%)
    pallas_call x1, Pallas kernels, body(): pl.pallas_call(functools.partial(kernel, (n_dp, n_branch, inner, slots, r...  75.4 us
    pallas_call x1, Pallas kernels, body(): pl.pallas_call(write_out, out_shape=tuple((jax.ShapeDtypeStruct(*x) for x...  2.57 us

profile of v3, /device:TPU:8, one launch (start us, length us, event | category | flops | bytes accessed | tf_op | source)
XLA Modules:
  0.0 78.6 jit_solution(7738074716917074173)
XLA Ops:
  0.6 75.4 %shard_map.170 = (bf16[8,32,4096]{2,1,0:T(8,128)(2,1)S(1)}, bf16[8,32,4096]{2,1,0:T(8,128)(2,1)S(1)}, bf16[8,32,512]{2,1,0:T(8,128)(2,1)S(1)}, bf16[8,32,512]{2,...) custom-call(bf16[512,512]{1,0:T(8,128)(2,1)} %bitcast.21, ...), custom_call_target="tpu_custom_call" | custom-call | tf_op jit(solution)/shard_map/pallas_call | solution.py:460
  76.0 2.6 %shard_map.171 = (bf16[8,32,4096]{2,1,0:T(8,128)(2,1)}, bf16[8,32,4096]{2,1,0:T(8,128)(2,1)}, bf16[8,32,512]{2,1,0:T(8,128)(2,1)}, bf16[8,32,512]{2,1,0:T(8,128)...) custom-call(bf16[8,32,4096]{2,1,0:T(8,128)(2,1)S(1)} %get-tuple-element.24.ref, ...), custom_call_target="tpu_custom_call" | custom-call | tf_op jit(solution)/shard_map/pallas_call | solution.py:505

commit v4 on v3

--- a/solution.py
+++ b/solution.py
@@ -30,13 +30,17 @@
     return vals * inv, inv
 
 
+def norm_back(scaled, normed):
+    return scaled - normed * jnp.mean(scaled * normed, axis=-1, keepdims=True)
+
+
 def kernel(
     dims,
-    pk, pv, q, rk, rv, g, q_gain, k_gain, lengths, prompts, owners,
-    attv, dqv, drkv, drvv, dpk, dpv, qg_out, kg_out,
+    pk, pv, q, rk, rv, g, q_gain, k_gain, lengths_in, prompts_in, owners_in,
+    attv, dqv, drkv, drvv, dpk, dpv, qg_out, kg_out, tail,
     qv, gv, rkv, rvv, kraw,
     kb0, kb1, kb2, kb3, vb0, vb1, vb2, vb3,
-    kt, vt, ck, cv, es, eb, ub, gq, gacc, rs_out, rs_in, ex1, ex2, ex3, ex4, meta,
+    kt, vt, ck, cv, es, eb, ub, gq, gacc, rs_out, rs_in, ex1, ex2, ex3, ex4, gains, lengths, prompts, owners, meta,
     ag_send, ag_recv, rs_send, rs_recv, gx_send, gx_recv, load_sem, ready,
 ):
     n_dp, n_branch, inner, slots, rows, heads, group, pre, hd = dims
@@ -76,11 +80,15 @@
     def _():
         for k in (1, 3, 2):
             tell(barrier, {"branch": k})
-        for _, _, extent, partner in stages:
-            for k in range(1, extent):
-                tell(barrier, partner(k))
-
-    def enter():
+
+    def greet_far():
+        @pl.when(me == 0)
+        def _():
+            for _, _, extent, partner in stages:
+                for k in range(1, extent):
+                    tell(barrier, partner(k))
+
+    def answer():
         @pl.when(me == 2)
         def _():
             pl.semaphore_wait(barrier, 3)
@@ -91,6 +99,7 @@
             pl.semaphore_wait(barrier, 2)
             tell(ready.at[0], {"branch": 0})
 
+    def enter():
         @pl.when(me == 0)
         def _():
             pl.semaphore_wait(ready.at[0], 2)
@@ -111,14 +120,30 @@
         pltpu.make_async_copy(src, dst, load_sem.at[base + i])
         for i, (src, dst) in enumerate(((q, qv), (g, gv), (rk, rkv), (rv, rvv)))
     ]
-    for h in range(heads):
+    small_loads = [
+        pltpu.make_async_copy(src, dst, load_sem.at[base + 4 + i])
+        for i, (src, dst) in enumerate(
+            (
+                (k_gain, gains.at[pl.ds(0, 1)]),
+                (q_gain, gains.at[pl.ds(8, 1)]),
+                (lengths_in, lengths),
+                (prompts_in, prompts),
+                (owners_in, owners),
+            )
+        )
+    ]
+    k_loads[0].start()
+    small_loads[0].start()
+    v_loads[0].start()
+    for copy in small_loads[1:]:
+        copy.start()
+    for h in range(1, heads):
         k_loads[h].start()
         v_loads[h].start()
     for copy in rest_loads:
         copy.start()
-
-    kg_row = k_gain[...]
-    qg_row = q_gain[...]
+    small_loads[0].wait()
+    kg_row = gains[0:1, :]
 
     def own_hat(h):
         k_loads[h].wait()
@@ -178,13 +203,16 @@
             rs(h, 4 + i).start()
 
     def rs_final(h):
+        normed, inv = norm_parts(kraw[h])
+        if h == heads - 1:
+            tail[1] = normed
         for i in range(2, 6):
             rs(h, i).wait_recv()
-        grad = rs_in[h, 3].astype(F32) + rs_in[h, 4].astype(F32)
-        normed, inv = norm_parts(kraw[h])
-        scaled = grad * kg_row
-        back = inv * (scaled - normed * jnp.mean(scaled * normed, axis=-1, keepdims=True))
-        dpk[:, h * hd : (h + 1) * hd] = back.astype(BF16)
+        scaled = (rs_in[h, 3].astype(F32) + rs_in[h, 4].astype(F32)) * (inv * kg_row)
+        if h == heads - 1:
+            tail[0] = scaled
+        else:
+            dpk[:, h * hd : (h + 1) * hd] = norm_back(scaled, normed).astype(BF16)
         dpv[:, h * hd : (h + 1) * hd] = (rs_in[h, 2].astype(F32) + rs_in[h, 5].astype(F32)).astype(BF16)
 
     def transposes(h):
@@ -266,15 +294,20 @@
 
         lax.fori_loop(0, slots // 2, step, 0)
 
+    answer()
     own_hat(0)
     enter()
     ag_direct(0)
+    greet_far()
     own_hat(1)
     ag_forward(0)
     ag_direct(1)
     for h in range(2, heads):
         own_hat(h)
 
+    for copy in small_loads[1:]:
+        copy.wait()
+    qg_row = gains[8:9, :]
     rels = []
     for s in range(slots):
         rel = owners[prompts[s]] - me
@@ -417,11 +450,19 @@
 
 
 def write_out(*refs):
-    count = len(refs) // 2
-    held, outs, sems = refs[:count], refs[count:-1], refs[-1]
-    copies = [pltpu.make_async_copy(a, b, sems.at[i]) for i, (a, b) in enumerate(zip(held, outs))]
+    count = (len(refs) - 3) // 2
+    held, last, outs, own, sems = refs[:count], refs[count], refs[count + 1 : -2], refs[-2], refs[-1]
+    early = held[4].shape[1] - own.shape[1]
+    pairs = list(zip(held, outs))
+    pairs[4] = (held[4].at[:, pl.ds(0, early)], outs[4].at[:, pl.ds(0, early)])
+    copies = [pltpu.make_async_copy(a, b, sems.at[i]) for i, (a, b) in enumerate(pairs)]
     for copy in copies:
         copy.start()
+    own[...] = norm_back(last[0], last[1]).astype(BF16)
+    copies.append(
+        pltpu.make_async_copy(own, outs[4].at[:, pl.ds(early, own.shape[1])], sems.at[count])
+    )
+    copies[-1].start()
     for copy in copies:
         copy.wait()
 
@@ -441,7 +482,6 @@
     cols = group * rows
     hbm = pl.BlockSpec(memory_space=pltpu.HBM)
     vmem = pl.BlockSpec(memory_space=pltpu.VMEM)
-    smem = pl.BlockSpec(memory_space=pltpu.SMEM)
 
     def held(dtype, *shape):
         return pltpu.VMEM(shape, dtype)
@@ -459,9 +499,9 @@
     )
     results = pl.pallas_call(
         functools.partial(kernel, (n_dp, n_branch, inner, slots, rows, heads, group, pre, hd)),
-        out_shape=tuple(pltpu.VMEM(*x) for x in shapes),
-        in_specs=[hbm] * 6 + [vmem] * 2 + [smem] * 3,
-        out_specs=(vmem,) * 8,
+        out_shape=tuple(pltpu.VMEM(*x) for x in shapes) + (pltpu.VMEM((2, pre, hd), F32),),
+        in_specs=[hbm] * 11,
+        out_specs=(vmem,) * 9,
         scratch_shapes=[
             held(BF16, slots, rows, qw),
             held(BF16, slots, rows, qw),
@@ -484,6 +524,10 @@
             held(F32, inner, 8, hd),
             held(F32, outer, 8, hd),
             held(F32, 8, hd),
+            held(F32, 16, hd),
+            pltpu.SMEM((slots,), jnp.int32),
+            pltpu.SMEM((slots,), jnp.int32),
+            pltpu.SMEM((n_branch,), jnp.int32),
             pltpu.SMEM((3, slots), jnp.int32),
             pltpu.SemaphoreType.DMA((heads, 6)),
             pltpu.SemaphoreType.DMA((heads, 6)),
@@ -491,11 +535,11 @@
             pltpu.SemaphoreType.DMA((heads, 6)),
             pltpu.SemaphoreType.DMA((4, 8)),
             pltpu.SemaphoreType.DMA((4, 8)),
-            pltpu.SemaphoreType.DMA((2 * heads + 4,)),
+            pltpu.SemaphoreType.DMA((2 * heads + 9,)),
             pltpu.SemaphoreType.REGULAR((2,)),
         ],
         compiler_params=pltpu.CompilerParams(
-            collective_id=0, has_side_effects=True, vmem_limit_bytes=int(58 * 1024 * 1024)
+            collective_id=0, has_side_effects=True, vmem_limit_bytes=57 * 1024 * 1024
         ),
     )(
         prefix_keys[0, 0], prefix_values[0, 0], resp_query[0, 0], resp_keys[0, 0],
@@ -505,9 +549,9 @@
     outs = pl.pallas_call(
         write_out,
         out_shape=tuple(jax.ShapeDtypeStruct(*x) for x in shapes),
-        in_specs=[vmem] * 8,
+        in_specs=[vmem] * 9,
         out_specs=(hbm,) * 8,
-        scratch_shapes=[pltpu.SemaphoreType.DMA((8,))],
+        scratch_shapes=[held(BF16, pre, hd), pltpu.SemaphoreType.DMA((9,))],
         compiler_params=pltpu.CompilerParams(vmem_limit_bytes=4 * 1024 * 1024),
     )(*results)
     return tuple(x[None, None] for x in outs[:6]) + (outs[6][0], outs[7][0])

time: 78.7 us -> 77.6 us (0.986)
  Pallas kernels: 77.9 us -> 76.6 us
    pallas_call x1, Pallas kernels: 75.4 us -> 74 us  [body(): pl.pallas_call(functools.partial(kernel, (n_dp, n_branch, inner, slots, r...]
where the time goes in v4:
time: 77.6 us; the launch traced here: 77.3 us
  Pallas kernels  76.6 us (99%)
    pallas_call x1, Pallas kernels, body(): pl.pallas_call(functools.partial(kernel, (n_dp, n_branch, inner, slots, r...  74 us
    pallas_call x1, Pallas kernels, body(): pl.pallas_call(write_out, out_shape=tuple((jax.ShapeDtypeStruct(*x) for x...  2.56 us

profile of v4, /device:TPU:8, one launch (start us, length us, event | category | flops | bytes accessed | tf_op | source)
XLA Modules:
  0.0 77.3 jit_solution(9564883988655912461)
XLA Ops:
  0.6 74.0 %shard_map.170 = (bf16[8,32,4096]{2,1,0:T(8,128)(2,1)S(1)}, bf16[8,32,4096]{2,1,0:T(8,128)(2,1)S(1)}, bf16[8,32,512]{2,1,0:T(8,128)(2,1)S(1)}, bf16[8,32,512]{2,...) custom-call(bf16[512,512]{1,0:T(8,128)(2,1)} %bitcast.21, ...), custom_call_target="tpu_custom_call" | custom-call | tf_op jit(solution)/shard_map/pallas_call | solution.py:500
  74.7 2.6 %shard_map.171 = (bf16[8,32,4096]{2,1,0:T(8,128)(2,1)}, bf16[8,32,4096]{2,1,0:T(8,128)(2,1)}, bf16[8,32,512]{2,1,0:T(8,128)(2,1)}, bf16[8,32,512]{2,1,0:T(8,128)...) custom-call(bf16[8,32,4096]{2,1,0:T(8,128)(2,1)S(1)} %get-tuple-element.25.ref, ...), custom_call_target="tpu_custom_call" | custom-call | tf_op jit(solution)/shard_map/pallas_call | solution.py:549

commit v5 on v4

--- a/solution.py
+++ b/solution.py
@@ -13,7 +13,6 @@
 F32 = jnp.float32
 BF16 = jnp.bfloat16
 LOG2E = math.log2(math.e)
-LN2 = math.log(2.0)
 
 
 def dot(a, b):
@@ -40,7 +39,7 @@
     attv, dqv, drkv, drvv, dpk, dpv, qg_out, kg_out, tail,
     qv, gv, rkv, rvv, kraw,
     kb0, kb1, kb2, kb3, vb0, vb1, vb2, vb3,
-    kt, vt, ck, cv, es, eb, ub, gq, gacc, rs_out, rs_in, ex1, ex2, ex3, ex4, gains, lengths, prompts, owners, meta,
+    kt, vt, ck, cv, es, ds, eb, ub, gq, gacc, rs_out, rs_in, ex1, ex2, ex3, ex4, gains, lengths, prompts, owners, meta,
     ag_send, ag_recv, rs_send, rs_recv, gx_send, gx_recv, load_sem, ready,
 ):
     n_dp, n_branch, inner, slots, rows, heads, group, pre, hd = dims
@@ -187,10 +186,8 @@
         return remote(rs_out.at[h, i], rs_in.at[h, i], rs_send.at[h, i], rs_recv.at[h, i], to)
 
     def rs_pack(h):
-        for i, (acc, scale, r) in enumerate(
-            ((ck, LN2, 2), (cv, 1.0, 2), (cv, 1.0, 1), (ck, LN2, 3), (ck, LN2, 1), (cv, 1.0, 3))
-        ):
-            rs_out[h, i] = (acc[meta[2, r]] * scale).astype(BF16)
+        for i, (acc, r) in enumerate(((ck, 2), (cv, 2), (cv, 1), (ck, 3), (ck, 1), (cv, 3))):
+            rs_out[h, i] = acc[meta[2, r]].astype(BF16)
 
     def rs_start(h):
         for i in range(4):
@@ -236,53 +233,56 @@
         q_inv = lax.rsqrt(jnp.mean(q_t * q_t, axis=0, keepdims=True) + EPSILON)
         q_n = q_t * q_inv
         gain = gq[...]
-        q_scaled = q_n * (gain * (LOG2E * score_scale))
-        q_low = q_scaled.astype(BF16)
+        q_low = (q_n * gain).astype(BF16)
         k_n, k_inv = norm_parts(rkv[s, :, h * hd : (h + 1) * hd])
         k_low = (k_n * kg_row).astype(BF16)
         v_low = rvv[s, :, h * hd : (h + 1) * hd]
 
         allowed = lax.broadcasted_iota(jnp.int32, (rows, cols), 0) <= token
-        e_r = jnp.where(allowed, jnp.exp2(dot(k_low, q_low)), 0.0)
+        e_r = jnp.where(allowed, jnp.exp2(dot(k_low, q_low) * (LOG2E * score_scale)), 0.0)
+        d_r = dot(v_low, g_low)
         total = jnp.sum(e_r, axis=0, keepdims=True)
+        mixed = jnp.sum(e_r * d_r, axis=0, keepdims=True)
         for c in range(pre // block):
             part = pl.ds(c * block, block)
-            e_c = jnp.exp2(dot(kb[h][rel, part, :], q_low))
+            e_c = jnp.exp2(dot(kb[h][rel, part, :], q_low) * (LOG2E * score_scale))
+            d_c = dot(vb[h][rel, part, :], g_low)
             es[u, part, :] = e_c
-            eb[u, part, :] = e_c.astype(BF16)
+            ds[u, part, :] = d_c
             total += jnp.sum(e_c, axis=0, keepdims=True)
+            mixed += jnp.sum(e_c * d_c, axis=0, keepdims=True)
         inv = 1.0 / total
-        e_r_low = e_r.astype(BF16)
-        o_t = (dot(vt[rel], eb[u]) + dot(v_low.T, e_r_low)) * inv
-        dots = jnp.sum(g_t * o_t, axis=0, keepdims=True)
+        mixed = mixed * inv
+        scaled_inv = inv * score_scale
+        p_r = (e_r * inv).astype(BF16)
+        u_r = (e_r * scaled_inv * (d_r - mixed)).astype(BF16)
+        for c in range(pre // block):
+            part = pl.ds(c * block, block)
+            e_c = es[u, part, :]
+            eb[u, part, :] = (e_c * inv).astype(BF16)
+            ub[u, part, :] = (e_c * scaled_inv * (ds[u, part, :] - mixed)).astype(BF16)
+
+        o_t = dot(vt[rel], eb[u]) + dot(v_low.T, p_r)
         o_low = jnp.where(live, o_t, 0.0).astype(BF16).T
         for i, a in enumerate(at):
             attv[s, :, a : a + hd] = o_low[i * rows : (i + 1) * rows, :]
-
-        u_r = (e_r * (dot(v_low, g_low) - dots)).astype(BF16)
-        for c in range(pre // block):
-            part = pl.ds(c * block, block)
-            d_c = dot(vb[h][rel, part, :], g_low)
-            ub[u, part, :] = (es[u, part, :] * (d_c - dots)).astype(BF16)
-        dq_t = (dot(kt[rel], ub[u]) + dot(k_low.T, u_r)) * (inv * score_scale)
-        gacc[...] += q_n * dq_t
+        dq_t = dot(kt[rel], ub[u]) + dot(k_low.T, u_r)
+        gacc[0] += q_n * dq_t
+        gacc[1] += q_low.astype(F32) * dq_t
         scaled = gain * dq_t
         back = q_inv * (scaled - q_n * jnp.mean(scaled * q_n, axis=0, keepdims=True))
         back_low = back.astype(BF16).T
         for i, a in enumerate(at):
             dqv[s, :, a : a + hd] = back_low[i * rows : (i + 1) * rows, :]
 
-        q_part = (q_scaled * inv).astype(BF16)
-        g_part = (g_t * inv).astype(BF16)
-        dk_r = dot_nt(u_r, q_part) * LN2
-        scaled_k = dk_r * kg_row
+        scaled_k = dot_nt(u_r, q_low) * kg_row
         back_k = k_inv * (scaled_k - k_n * jnp.mean(scaled_k * k_n, axis=-1, keepdims=True))
         drkv[s, :, h * hd : (h + 1) * hd] = back_k.astype(BF16)
-        drvv[s, :, h * hd : (h + 1) * hd] = dot_nt(e_r_low, g_part).astype(BF16)
+        drvv[s, :, h * hd : (h + 1) * hd] = dot_nt(p_r, g_low).astype(BF16)
         for c in range(pre // block):
             part = pl.ds(c * block, block)
-            ck[s, part, :] = ck[prev, part, :] + dot_nt(ub[u, part, :], q_part)
-            cv[s, part, :] = cv[prev, part, :] + dot_nt(eb[u, part, :], g_part)
+            ck[s, part, :] = ck[prev, part, :] + dot_nt(ub[u, part, :], q_low)
+            cv[s, part, :] = cv[prev, part, :] + dot_nt(eb[u, part, :], g_low)
 
     def run_head(h, events):
         def step(i, carry):
@@ -349,10 +349,9 @@
         if h + 1 < heads:
             rs_pack(h)
 
-    def spread(value):
-        return jnp.broadcast_to(value, (8, hd))
-
-    ex1[me] = spread(jnp.sum(gacc[...].T, axis=0, keepdims=True))
+    for i in range(2):
+        ex1[me, i : i + 1, :] = jnp.sum(gacc[i].T, axis=0, keepdims=True)
+    ex1[me, 2:8, :] = jnp.zeros((6, hd), F32)
 
     def gain_copy(src, dst, i, k, j, to):
         return pltpu.make_async_remote_copy(
@@ -427,9 +426,8 @@
     def _():
         down(me).wait_recv()
 
-    value = ex4[0:1, :]
-    qg_out[...] = value
-    kg_out[...] = value * qg_row / kg_row
+    qg_out[...] = ex4[0:1, :]
+    kg_out[...] = ex4[1:2, :] / kg_row
 
     for h in range(heads):
         for i in range(6):
@@ -514,10 +512,11 @@
             held(F32, slots + 1, pre, hd),
             held(F32, slots + 1, pre, hd),
             held(F32, 2, pre, cols),
+            held(F32, 2, pre, cols),
             held(BF16, 2, pre, cols),
             held(BF16, 2, pre, cols),
             held(F32, hd, cols),
-            held(F32, hd, cols),
+            held(F32, 2, hd, cols),
             held(BF16, heads, 6, pre, hd),
             held(BF16, heads, 6, pre, hd),
             held(F32, n_branch, 8, hd),

time: 77.6 us -> 77.6 us (level)
  no operation moved by 1% of the time
where the time goes in v5:
time: 77.6 us; the launch traced here: 77.3 us
  Pallas kernels  76.6 us (99%)
    pallas_call x1, Pallas kernels, body(): pl.pallas_call(functools.partial(kernel, (n_dp, n_branch, inner, slots, r...  74 us
    pallas_call x1, Pallas kernels, body(): pl.pallas_call(write_out, out_shape=tuple((jax.ShapeDtypeStruct(*x) for x...  2.56 us

profile of v5, /device:TPU:8, one launch (start us, length us, event | category | flops | bytes accessed | tf_op | source)
XLA Modules:
  0.0 77.3 jit_solution(14979618257611757194)
XLA Ops:
  0.6 74.0 %shard_map.170 = (bf16[8,32,4096]{2,1,0:T(8,128)(2,1)S(1)}, bf16[8,32,4096]{2,1,0:T(8,128)(2,1)S(1)}, bf16[8,32,512]{2,1,0:T(8,128)(2,1)S(1)}, bf16[8,32,512]{2,...) custom-call(bf16[512,512]{1,0:T(8,128)(2,1)} %bitcast.21, ...), custom_call_target="tpu_custom_call" | custom-call | tf_op jit(solution)/shard_map/pallas_call | solution.py:498
  74.7 2.6 %shard_map.171 = (bf16[8,32,4096]{2,1,0:T(8,128)(2,1)}, bf16[8,32,4096]{2,1,0:T(8,128)(2,1)}, bf16[8,32,512]{2,1,0:T(8,128)(2,1)}, bf16[8,32,512]{2,1,0:T(8,128)...) custom-call(bf16[8,32,4096]{2,1,0:T(8,128)(2,1)S(1)} %get-tuple-element.25.ref, ...), custom_call_target="tpu_custom_call" | custom-call | tf_op jit(solution)/shard_map/pallas_call | solution.py:548

commit v6 on v5

--- a/solution.py
+++ b/solution.py
@@ -66,11 +66,6 @@
     def tell(sem, to):
         pl.semaphore_signal(sem, inc=1, device_id=to, device_id_type=MESH)
 
-    @pl.when(me == 2)
-    def _():
-        tell(barrier, {"branch": 1})
-        tell(barrier, {"branch": 3})
-
     @pl.when((me == 1) | (me == 3))
     def _():
         tell(barrier, {"branch": 2})
@@ -91,17 +86,14 @@
         @pl.when(me == 2)
         def _():
             pl.semaphore_wait(barrier, 3)
+            for k in (1, 3):
+                tell(ready.at[0], {"branch": k})
             tell(ready.at[1], {"branch": 0})
 
         @pl.when((me == 1) | (me == 3))
         def _():
-            pl.semaphore_wait(barrier, 2)
+            pl.semaphore_wait(barrier, 1)
             tell(ready.at[0], {"branch": 0})
-
-    def enter():
-        @pl.when(me == 0)
-        def _():
-            pl.semaphore_wait(ready.at[0], 2)
 
     def head_cols(h):
         return pl.ds(h * hd, hd)
@@ -167,9 +159,30 @@
         )[i]
         return remote(src, dst, ag_send.at[h, i], ag_recv.at[h, i], to)
 
-    def ag_direct(h):
-        for i in range(4):
+    def ag_direct(h, parts=(0, 1, 2, 3)):
+        for i in parts:
             ag(h, i).start()
+
+    def ag_enter():
+        @pl.when(me == 0)
+        def _():
+            pl.semaphore_wait(ready.at[0], 2)
+
+        @pl.when(me == 1)
+        def _():
+            ag_direct(0, (1, 3))
+            pl.semaphore_wait(ready.at[0], 1)
+            ag_direct(0, (0, 2))
+
+        @pl.when(me == 3)
+        def _():
+            ag_direct(0, (0, 2))
+            pl.semaphore_wait(ready.at[0], 1)
+            ag_direct(0, (1, 3))
+
+        @pl.when((me == 0) | (me == 2))
+        def _():
+            ag_direct(0)
 
     def ag_forward(h):
         ag(h, 0).wait_recv()
@@ -183,34 +196,37 @@
 
     def rs(h, i):
         to = right if i % 2 == 0 else left
-        return remote(rs_out.at[h, i], rs_in.at[h, i], rs_send.at[h, i], rs_recv.at[h, i], to)
+        part = pl.ds(2 * i, 2) if i < 2 else i + 2
+        return remote(rs_out.at[h, part], rs_in.at[h, part], rs_send.at[h, i], rs_recv.at[h, i], to)
 
     def rs_pack(h):
-        for i, (acc, r) in enumerate(((ck, 2), (cv, 2), (cv, 1), (ck, 3), (ck, 1), (cv, 3))):
+        for i, (acc, r) in enumerate(((ck, 2), (cv, 1), (cv, 2), (ck, 3), (ck, 1), (cv, 3))):
             rs_out[h, i] = acc[meta[2, r]].astype(BF16)
 
     def rs_start(h):
-        for i in range(4):
+        for i in range(2):
             rs(h, i).start()
 
     def rs_second(h):
         for i in (0, 1):
             rs(h, i).wait_recv()
-            rs_out[h, 4 + i] = (rs_out[h, 4 + i].astype(F32) + rs_in[h, i].astype(F32)).astype(BF16)
-            rs(h, 4 + i).start()
+            rs_out[h, 4 + i] = (
+                rs_out[h, 4 + i].astype(F32) + rs_in[h, 2 * i].astype(F32)
+            ).astype(BF16)
+            rs(h, 2 + i).start()
 
     def rs_final(h):
         normed, inv = norm_parts(kraw[h])
         if h == heads - 1:
             tail[1] = normed
-        for i in range(2, 6):
+        for i in range(2, 4):
             rs(h, i).wait_recv()
         scaled = (rs_in[h, 3].astype(F32) + rs_in[h, 4].astype(F32)) * (inv * kg_row)
         if h == heads - 1:
             tail[0] = scaled
         else:
             dpk[:, h * hd : (h + 1) * hd] = norm_back(scaled, normed).astype(BF16)
-        dpv[:, h * hd : (h + 1) * hd] = (rs_in[h, 2].astype(F32) + rs_in[h, 5].astype(F32)).astype(BF16)
+        dpv[:, h * hd : (h + 1) * hd] = (rs_in[h, 1].astype(F32) + rs_in[h, 5].astype(F32)).astype(BF16)
 
     def transposes(h):
         for r in range(1, n_branch):
@@ -296,8 +312,7 @@
 
     answer()
     own_hat(0)
-    enter()
-    ag_direct(0)
+    ag_enter()
     greet_far()
     own_hat(1)
     ag_forward(0)
@@ -432,6 +447,7 @@
     for h in range(heads):
         for i in range(6):
             ag(h, i).wait_send()
+        for i in range(4):
             rs(h, i).wait_send()
 
     @pl.when(me != 0)

time: 77.6 us -> 79.1 us (1.019)
  Pallas kernels: 76.6 us -> 78.4 us
    pallas_call x1, Pallas kernels: 74 us -> 75.8 us  [body(): pl.pallas_call(functools.partial(kernel, (n_dp, n_branch, inner, slots, r...]
where the time goes in v6:
time: 79.1 us; the launch traced here: 79 us
  Pallas kernels  78.4 us (99%)
    pallas_call x1, Pallas kernels, body(): pl.pallas_call(functools.partial(kernel, (n_dp, n_branch, inner, slots, r...  75.8 us
    pallas_call x1, Pallas kernels, body(): pl.pallas_call(write_out, out_shape=tuple((jax.ShapeDtypeStruct(*x) for x...  2.56 us

profile of v6, /device:TPU:8, one launch (start us, length us, event | category | flops | bytes accessed | tf_op | source)
XLA Modules:
  0.0 79.0 jit_solution(17536675583640797088)
XLA Ops:
  0.6 75.8 %shard_map.170 = (bf16[8,32,4096]{2,1,0:T(8,128)(2,1)S(1)}, bf16[8,32,4096]{2,1,0:T(8,128)(2,1)S(1)}, bf16[8,32,512]{2,1,0:T(8,128)(2,1)S(1)}, bf16[8,32,512]{2,...) custom-call(bf16[512,512]{1,0:T(8,128)(2,1)} %bitcast.21, ...), custom_call_target="tpu_custom_call" | custom-call | tf_op jit(solution)/shard_map/pallas_call | solution.py:514
  76.4 2.6 %shard_map.171 = (bf16[8,32,4096]{2,1,0:T(8,128)(2,1)}, bf16[8,32,4096]{2,1,0:T(8,128)(2,1)}, bf16[8,32,512]{2,1,0:T(8,128)(2,1)}, bf16[8,32,512]{2,1,0:T(8,128)...) custom-call(bf16[8,32,4096]{2,1,0:T(8,128)(2,1)S(1)} %get-tuple-element.25.ref, ...), custom_call_target="tpu_custom_call" | custom-call | tf_op jit(solution)/shard_map/pallas_call | solution.py:564
